TPU v7x, 32 devices: a whole 2x2x4 slice. The times are simulated.
32 devices in a mesh: seq: 8 (over y, x, core), tp: 4 (over z).
Axes of the slice: x: 2, y: 2, z: 4, core: 2. Of those that a mesh axis runs over, the one named last changes fastest.
Arguments:
- vis_feat: bfloat16 [128, 12800], P('seq', 'tp'), may hold values from -256 to 256
- ln_gain: float32 [12800], P('tp'), may hold values from 0.25 to 1.75
- proj_weight: bfloat16 [12800, 8192], P('tp', 'seq'), may hold values from -0.0546875 to 0.0546875
- text_embed: bfloat16 [2048, 8192], P('seq'), may hold values from -128 to 128
- rms_gain: float32 [8192], replicated, may hold values from 0.25 to 1.75
- wq: bfloat16 [8192, 4096], P('seq', 'tp'), may hold values from -1 to 1
- wk: bfloat16 [8192, 1024], P('seq', 'tp'), may hold values from -1 to 1
- wv: bfloat16 [8192, 1024], P('seq', 'tp'), may hold values from -0.0625 to 0.0625
- doc_ids: int32 [2048], P('seq'), may hold values from 0 to 15, as said below
- vis_slot: int32 [2048], P('seq'), may hold values from -1 to 31, as said below
- slot_token: int32 [256], replicated, may hold values from -1 to 127, as said below
- token_slot: int32 [128], replicated, may hold values from 0 to 255, as said below
- cotangent: bfloat16 [2048, 4096], P('seq', 'tp'), may hold values from -6 to 6
Outputs:
- context: bfloat16 [2048, 4096], P('seq', 'tp')
- vis_grad: bfloat16 [128, 12800], P('seq', 'tp')
Inputs may be any that keep to these rules, and one draw needn't show every extreme that they name: `doc_ids`: document numbers never fall along the positions and rise by one at each new document; each document has 1 to 256 positions, and one has exactly 256. `vis_slot`: in each block of 256 positions the image positions form one run that ends at the block's last position, numbered 0, 1, 2 ... in order; a block has 0 to 32 of them, 128 in all, and some block has exactly 32. `slot_token`: entry b * 32 + j names the visual token at image position j of block b, or -1 where block b has fewer image positions; each visual token is named once. `token_slot`: for each visual token, the index of the entry of slot_token that names it.
All inputs are finite; a program needn't handle non-finite values.
Results may differ from a plain program's by a relative error of at most 0.025.
Values may be sent and summed in bfloat16 or wider, within the bound.
A program may use at most 128 MiB of HBM per device.

v0:
```python
import math

import jax
import jax.numpy as jnp
from jax import lax
from jax.sharding import PartitionSpec as P

VF = 12800
HEAD = 128
CAPD = 32
GROUP = 4


ln_eps = 1e-05
rms_eps = 1e-06
rope_base = 1000000.0
masked_score = -1e30


def shifted(x, axis, by):
    peers = lax.axis_size(axis)
    pairs = [(i, i + by) for i in range(peers) if 0 <= i + by < peers]
    return lax.ppermute(x, axis, pairs)


def rope_tables(positions, head_width):
    half = head_width // 2
    frequency = rope_base ** (-(jnp.arange(half).astype(jnp.float32) * 2.0 / head_width))
    angle = positions.astype(jnp.float32)[:, None] * frequency[None, :]
    return (jnp.cos(angle), jnp.sin(angle))


def rotate(values, cosine, sine):
    half = values.shape[-1] // 2
    first = values[..., :half]
    second = values[..., half:]
    cos_rows = cosine[:, None, :]
    sin_rows = sine[:, None, :]
    return jnp.concatenate(
        [first * cos_rows - second * sin_rows, second * cos_rows + first * sin_rows], axis=-1
    )


def unrotate(grads, cosine, sine):
    half = grads.shape[-1] // 2
    first = grads[..., :half]
    second = grads[..., half:]
    cos_rows = cosine[:, None, :]
    sin_rows = sine[:, None, :]
    return jnp.concatenate(
        [first * cos_rows + second * sin_rows, second * cos_rows - first * sin_rows], axis=-1
    )


def norm_backward(rows, grads, gain):
    inv_rms = lax.rsqrt(jnp.mean(rows * rows, axis=1, keepdims=True) + rms_eps)
    scaled = grads * gain[None, :]
    inner = jnp.mean(rows * scaled, axis=1, keepdims=True)
    return inv_rms * scaled - rows * (inv_rms * inv_rms * inv_rms) * inner


def attention_block(queries, keys, values, grads, allowed):
    scale = 1.0 / math.sqrt(queries.shape[-1])
    scores = jnp.einsum("qhgd,khd->hgqk", queries, keys, preferred_element_type=jnp.float32) * scale
    masked = jnp.where(allowed[None, None], scores, masked_score)
    peak = jnp.max(masked, axis=-1, keepdims=True)
    raised = jnp.where(allowed[None, None], jnp.exp(masked - peak), 0.0)
    shares = raised / jnp.sum(raised, axis=-1, keepdims=True)
    shares_low = shares.astype(jnp.bfloat16)
    context = jnp.einsum(
        "hgqk,khd->qhgd", shares_low, values, preferred_element_type=jnp.float32
    ).astype(jnp.bfloat16)
    share_grads = jnp.einsum("qhgd,khd->hgqk", grads, values, preferred_element_type=jnp.float32)
    delta = jnp.sum(shares * share_grads, axis=-1, keepdims=True)
    score_grads = (shares * (share_grads - delta) * scale).astype(jnp.bfloat16)
    query_grads = jnp.einsum(
        "hgqk,khd->qhgd", score_grads, keys, preferred_element_type=jnp.float32
    )
    key_grads = jnp.einsum(
        "hgqk,qhgd->khd", score_grads, queries, preferred_element_type=jnp.float32
    )
    value_grads = jnp.einsum(
        "hgqk,qhgd->khd", shares_low, grads, preferred_element_type=jnp.float32
    )
    return (context, query_grads, key_grads, value_grads)


def on_device(
    vis_feat,
    ln_gain,
    proj_weight,
    text_embed,
    rms_gain,
    wq,
    wk,
    wv,
    doc_ids,
    vis_slot,
    slot_token,
    token_slot,
    cotangent,
):
    seq_count = lax.axis_size("seq")
    my_index = lax.axis_index("seq")
    tok_rows = text_embed.shape[0]
    slot_cols = proj_weight.shape[1]
    features = vis_feat.astype(jnp.float32)
    row_total, row_squares = lax.psum(
        (jnp.sum(features, axis=1), jnp.sum(features * features, axis=1)), "tp"
    )
    row_mean = row_total / VF
    row_var = row_squares / VF - row_mean * row_mean
    inv_std = lax.rsqrt(row_var + ln_eps)
    centred = (features - row_mean[:, None]) * inv_std[:, None]
    vis_normed = (centred * ln_gain[None, :]).astype(jnp.bfloat16)
    partial_embed = jnp.dot(
        lax.all_gather(vis_normed, "seq", axis=0, tiled=True),
        proj_weight,
        preferred_element_type=jnp.float32,
    )
    slot_live = (slot_token >= 0)[:, None]
    slot_index = jnp.maximum(slot_token, 0)
    summed = lax.psum(partial_embed, "tp")
    embed_rows = jnp.take(summed.astype(jnp.bfloat16), slot_index, axis=0)
    outgoing = jnp.where(slot_live, embed_rows, jnp.zeros_like(embed_rows)).reshape(
        seq_count, CAPD, slot_cols
    )
    arrived = lax.all_to_all(outgoing, "seq", split_axis=0, concat_axis=2, tiled=True)[0]
    lanes = jnp.arange(CAPD, dtype=jnp.int32)
    one_hot = (vis_slot[:, None] == lanes[None, :]).astype(jnp.bfloat16)
    placed = jnp.dot(one_hot, arrived, preferred_element_type=jnp.float32).astype(jnp.bfloat16)
    is_image = vis_slot >= 0
    hidden = jnp.where(is_image[:, None], placed, text_embed)
    hidden_wide = hidden.astype(jnp.float32)
    inv_rms = lax.rsqrt(jnp.mean(hidden_wide * hidden_wide, axis=1, keepdims=True) + rms_eps)
    normed = (hidden_wide * inv_rms * rms_gain[None, :]).astype(jnp.bfloat16)
    stacked = jnp.concatenate([wq, wk, wv], axis=1)
    query_cols = wq.shape[1]
    key_cols = wk.shape[1]
    gathered = lax.all_gather(stacked, "seq", axis=0, tiled=True)
    projected = jnp.dot(normed, gathered, preferred_element_type=jnp.float32)
    local_heads = query_cols // HEAD
    local_groups = key_cols // HEAD
    positions = my_index * tok_rows + jnp.arange(tok_rows, dtype=jnp.int32)
    cosine, sine = rope_tables(positions, HEAD)
    queries = rotate(
        projected[:, :query_cols].reshape(tok_rows, local_heads, HEAD), cosine, sine
    ).astype(jnp.bfloat16)
    keys = rotate(
        projected[:, query_cols : query_cols + key_cols].reshape(tok_rows, local_groups, HEAD),
        cosine,
        sine,
    ).astype(jnp.bfloat16)
    values = (
        projected[:, query_cols + key_cols :]
        .astype(jnp.bfloat16)
        .reshape(tok_rows, local_groups, HEAD)
    )
    doc_marks = (doc_ids + 1).astype(jnp.bfloat16)
    prev_keys, prev_values, prev_docs = shifted((keys, values, doc_marks), "seq", 1)
    all_keys = jnp.concatenate([prev_keys, keys], axis=0)
    all_values = jnp.concatenate([prev_values, values], axis=0)
    query_docs = doc_marks.astype(jnp.float32)
    key_docs = jnp.concatenate([prev_docs.astype(jnp.float32), query_docs], axis=0)
    key_positions = jnp.concatenate([positions - tok_rows, positions], axis=0)
    allowed = (key_docs[None, :] == query_docs[:, None]) & (
        key_positions[None, :] <= positions[:, None]
    )
    grads = cotangent.reshape(tok_rows, local_groups, GROUP, HEAD)
    context, query_grads, key_grads, value_grads = attention_block(
        queries.reshape(tok_rows, local_groups, GROUP, HEAD), all_keys, all_values, grads, allowed
    )
    back_keys, back_values = (
        shifted(key_grads[:tok_rows].astype(jnp.bfloat16), "seq", -1).astype(jnp.float32),
        shifted(value_grads[:tok_rows].astype(jnp.bfloat16), "seq", -1).astype(jnp.float32),
    )
    key_total = key_grads[tok_rows:] + back_keys
    value_total = value_grads[tok_rows:] + back_values
    query_pre = (
        unrotate(query_grads.reshape(tok_rows, local_heads, HEAD), cosine, sine)
        .astype(jnp.bfloat16)
        .reshape(tok_rows, query_cols)
    )
    key_pre = unrotate(key_total, cosine, sine).astype(jnp.bfloat16).reshape(tok_rows, key_cols)
    value_pre = value_total.astype(jnp.bfloat16).reshape(tok_rows, key_cols)
    proj_grads = jnp.concatenate([query_pre, key_pre, value_pre], axis=1)
    selected = lax.dot_general(
        one_hot, proj_grads, (((0,), (0,)), ((), ())), preferred_element_type=jnp.float32
    ).astype(jnp.bfloat16)
    norm_part = lax.dot_general(
        selected, gathered, (((1,), (1,)), ((), ())), preferred_element_type=jnp.float32
    )
    norm_grads = lax.psum(norm_part.astype(jnp.bfloat16), "tp").astype(jnp.float32)
    embed_grads = norm_backward(arrived.astype(jnp.float32), norm_grads, rms_gain).astype(
        jnp.bfloat16
    )
    returned = lax.all_to_all(embed_grads[None], "seq", split_axis=2, concat_axis=0, tiled=True)
    token_grads = jnp.take(returned.reshape(seq_count * CAPD, slot_cols), token_slot, axis=0)
    own_rows = vis_feat.shape[0]
    whole_grads = lax.psum(
        lax.dot_general(
            token_grads, proj_weight, (((1,), (1,)), ((), ())), preferred_element_type=jnp.float32
        ).astype(jnp.bfloat16),
        "seq",
    ).astype(jnp.float32)
    feature_grads = lax.dynamic_slice_in_dim(whole_grads, my_index * own_rows, own_rows, 0)
    scaled = feature_grads * ln_gain[None, :]
    grad_total, grad_inner = lax.psum(
        (jnp.sum(scaled, axis=1), jnp.sum(scaled * centred, axis=1)), "tp"
    )
    vis_grad = (
        inv_std[:, None]
        * (scaled - (grad_total / VF)[:, None] - centred * (grad_inner / VF)[:, None])
    ).astype(jnp.bfloat16)
    return (context.reshape(tok_rows, query_cols), vis_grad)


def solution(mesh):
    return jax.shard_map(
        on_device,
        mesh=mesh,
        in_specs=(
            P("seq", "tp"),
            P("tp"),
            P("tp", "seq"),
            P("seq", None),
            P(),
            P("seq", "tp"),
            P("seq", "tp"),
            P("seq", "tp"),
            P("seq"),
            P("seq"),
            P(),
            P(),
            P("seq", "tp"),
        ),
        out_specs=(P("seq", "tp"), P("seq", "tp")),
        check_vma=False,
    )
```

profile of v0, /device:TPU:0, one launch (start us, length us, event | category | flops | bytes accessed | tf_op | source)
XLA Modules:
  0.0 432.2 jit_solution(12028385693535699696)
XLA Ops:
  7.3 3.2 pad_maximum_fusion
  10.5 2.4 collective-permute-start.1
  13.2 12.8 %all-reduce.1 = (f32[16]{0:T(128)S(1)}, f32[16]{0:T(128)S(1)}) all-reduce(f32[16]{0:T(128)S(1)} %get-tuple-element.13, f32[16]{0:T(128)S(1)} %get-tuple-element.12), channel_id=1, replica_groups=mesh['seq'=8,'tp'=4] {'tp'}, use_global_device_ids=true, to_apply=%region_3.0 | all-reduce | flops 32 | bytes 256 | tf_op jit(solution)/shard_map/psum | solution.py:108
  26.1 15.1 %all_gather.6 = bf16[128,3200]{1,0:T(8,128)(2,1)S(1)} all-gather(bf16[16,3200]{1,0:T(8,128)(2,1)S(1)} %fusion.47), channel_id=1, replica_groups=mesh['seq'=8,'tp'=4] {'seq'}, dimensions={0}, use_global_device_ids=true | all-gather | bytes 921600 | tf_op jit(solution)/shard_map/all_gather | solution.py:117
  41.2 4.0 fusion.76
  45.3 28.4 %all-reduce.9 = bf16[128,1024]{1,0:T(8,128)(2,1)S(1)} all-reduce(f32[128,1024]{1,0:T(8,128)S(1)} %fusion.76), channel_id=1, replica_groups=mesh['seq'=8,'tp'=4] {'tp'}, use_global_device_ids=true, to_apply=%region_4.0 | all-reduce | flops 131072 | bytes 786432 | tf_op jit(solution)/shard_map/psum | solution.py:123
  73.7 1.2 gather_fusion
  74.9 0.9 select_select_fusion
  75.8 3.5 all-to-all-start
  79.4 0.5 multiply_cosine_fusion
  80.0 1.0 copy.135
  81.0 0.9 compare_and_fusion
  81.9 13.0 %all-to-all-done = bf16[8,32,1024]{2,1,0:T(8,128)(2,1)S(1)} async-done(((bf16[8,32,1024]{2,1,0:T(8,128)(2,1)}), bf16[8,32,1024]{2,1,0:T(8,128)(2,1)S(1)}, u32[]{:S(2)}, u32[]{:S(2)}) %all-to-all-start) | async-done | bytes 524320 | tf_op jit(solution)/shard_map/all_to_all | solution.py:128
  95.0 4.8 %fusion.3 = (f32[256]{0:T(256)S(1)}, bf16[256,8192]{1,0:T(8,128)(2,1)}) fusion(bf16[256,8192]{1,0:T(8,128)(2,1)} %param.16, bf16[32,8192]{1,0:T(8,128)(2,1)S(1)} %bitcast.123, s32[256]{0:T(256)S(1)} %copy-done.12, pred[256]{0:T(512)(128)(4,1)S(1)} %broadcast_compare_fusion.2), kind=kOutput, calls=%fused_computation.9 | convolution fusion | flops 144711424 | bytes 8915200 | tf_op jit(solution)/shard_map/dot_general | solution.py:131
  99.8 47.7 %all-gather.2.cloned.1.call-done = bf16[8192,1536]{1,0:T(8,128)(2,1)} async-done(((bf16[1024,1536]{1,0:T(8,128)(2,1)}), bf16[8192,1536]{1,0:T(8,128)(2,1)}) %all-gather.2.cloned.1.call-update) | async-done | bytes 25165840 | tf_op jit(solution)/shard_map/all_gather | solution.py:140
  147.5 12.8 %fusion.6 = f32[256,1536]{1,0:T(8,128)S(1)} fusion(bf16[8192,1536]{1,0:T(8,128)(2,1)} %all-gather.2.cloned.1.call-done, bf16[256,8192]{1,0:T(8,128)(2,1)} %get-tuple-element.41, f32[8192]{0:T(1024)S(1)} %copy-done.10, f32[256]{0:T(256)S(1)} %add_rsqrt_fusion), kind=kOutput, calls=%fused_computation.13 | convolution fusion | flops 6450839552 | bytes 30966784 | tf_op jit(solution)/shard_map/dot_general | solution.py:141
  160.3 0.7 slice.68
  161.1 0.7 copy.130
  161.9 2.8 collective-permute-start
  164.9 1.1 reshape.219
  166.0 0.3 fusion.74
  166.5 2.8 collective-permute-start.2
  169.3 0.4 subtract_convert_fusion.1
  170.1 0.6 copy-done.15
  170.8 5.1 %fusion.75 = (f32[2,4,256]{2,1,0:T(4,128)S(1)}, f32[2,4,256,512]{2,3,1,0:T(8,128)}) fusion(pred[256,512]{0,1:T(8,128)(4,1)} %compare_and_fusion, bf16[256,2,64]{2,0,1:T(8,128)(2,1)} %copy-done.5, bf16[256,2,64]{2,0,1:T(8,128)(2,1)} %copy-done.3, bf16[256,2,128]{2,0,1:T(8,128)(2,1)} %copy-done.15, bf16[256,2,4,64]{3,0,2,1:T(8,128)(2,1)S(1)} %bitcast.137, ...), kind=kOutput, calls=%fused_computation.138 | convolution fusion | flops 275513856 | bytes 5120000 | tf_op jit(solution)/shard_map/sub | solution.py:67
  175.9 3.0 convolution_bitcast_fusion
  178.9 0.7 slice.98
  179.6 1.3 collective-permute-start.4
  180.9 3.7 fusion.54
  184.6 8.3 %fusion.20 = f32[512,2,128]{2,0,1:T(8,128)} fusion(f32[2,512,256,4]{2,1,3,0:T(8,128)} %fusion.54, bf16[256,2,4,64]{3,0,2,1:T(8,128)(2,1)S(1)} %bitcast.138, bf16[256,2,4,64]{3,0,2,1:T(8,128)(2,1)S(1)} %bitcast.136, f32[2,4,256,512]{2,3,1,0:T(8,128)} %get-tuple-element.43, f32[2,4,256]{2,1,0:T(4,128)S(1)} %get-tuple-element.42), kind=kOutput, calls=%fused_computation.36 | convolution fusion | flops 276826624 | bytes 9445376 | tf_op jit(solution)/shard_map/hgqk,qhgd->khd/dot_general | solution.py:79
  192.9 7.0 %fusion.19 = f32[2,128,4,256]{3,1,2,0:T(8,128)S(1)} fusion(f32[2,512,256,4]{2,1,3,0:T(8,128)} %fusion.54, bf16[256,2,64]{2,0,1:T(8,128)(2,1)S(1)} %copy-done.6, bf16[256,2,64]{2,0,1:T(8,128)(2,1)S(1)} %copy-done.4, bf16[256,2,128]{2,0,1:T(8,128)(2,1)S(1)} %copy-done.16, f32[2,4,256,512]{2,3,1,0:T(8,128)} %get-tuple-element.43, ...), kind=kOutput, calls=%fused_computation.32 | convolution fusion | flops 276564480 | bytes 9707520 | tf_op jit(solution)/shard_map/hgqk,khd->qhgd/dot_general | solution.py:76
  199.9 0.9 fusion.73
  200.8 1.6 slice.99
  202.5 1.5 collective-permute-start.3
  204.0 0.4 copy.134
  204.4 1.5 copy.133
  205.9 0.3 add_convert_fusion
  206.2 0.3 pad_maximum_fusion.2
  206.6 0.3 copy-done.8
  206.9 0.9 fusion.40
  208.0 1.0 slice_add_fusion.1
  209.5 13.2 %convolution_convert_fusion.1 = bf16[32,8192]{1,0:T(8,128)(2,1)} fusion(bf16[8192,1536]{1,0:T(8,128)(2,1)} %all-gather.2.cloned.1.call-done, bf16[256,256]{1,0:T(8,128)(2,1)S(1)} %copy.109, bf16[256,256]{1,0:T(8,128)(2,1)S(1)} %copy.108, bf16[256,1024]{1,0:T(8,128)(2,1)S(1)} %bitcast.127, s32[256]{0:T(256)S(1)} %copy-done.12), kind=kOutput, calls=%fused_computation.8 | convolution fusion | flops 833150976 | bytes 26477568 | tf_op jit(solution)/shard_map/dot_general | solution.py:190
  223.0 43.1 %all-reduce.6.cloned.1.call-done = bf16[32,8192]{1,0:T(8,128)(2,1)} async-done(((bf16[32,8192]{1,0:T(8,128)(2,1)}), bf16[32,8192]{1,0:T(8,128)(2,1)}) %all-reduce.6.cloned.1.call-update) | async-done | bytes 524304 | tf_op jit(solution)/shard_map/psum | solution.py:193
  266.1 1.3 fusion.24
  267.4 1.3 fusion.37
  268.7 6.7 %copy.110 = bf16[1,32,8192]{1,0,2:T(2,128)(2,1)} copy(bf16[1,32,8192]{2,1,0:T(8,128)(2,1)S(1)} %fusion.37) | data formatting | bytes 1048576 | tf_op jit(solution)/shard_map/broadcast_in_dim | solution.py:197
  275.5 0.5 broadcast.216
  276.0 45.2 %reduce.1 = bf16[8192,32]{1,0:T(8,128)(2,1)S(1)} reduce(bf16[8192,1,32]{2,1,0:T(2,128)(2,1)} %bitcast.119, bf16[]{:T(256)} %broadcast.216), dimensions={1}, to_apply=%bitcast.101.reduce_sub_computation | reduce | bytes 1048578
  321.2 2.7 reshape.250
  323.9 3.7 all-to-all-start.1
  327.6 0.3 all-reduce.8.cloned.1.call-start
  327.9 9.4 %all-to-all-done.1 = bf16[8,2,16384]{2,1,0:T(2,128)(2,1)S(1)} async-done(((bf16[8,2,16384]{2,1,0:T(2,128)(2,1)}), bf16[8,2,16384]{2,1,0:T(2,128)(2,1)S(1)}, u32[]{:S(2)}, u32[]{:S(2)}) %all-to-all-start.1) | async-done | bytes 524320 | tf_op jit(solution)/shard_map/all_to_all | solution.py:197
  337.3 4.5 %reshape.251 = bf16[8192,1,32]{2,1,0:T(2,128)(2,1)} reshape(bf16[8,2,16384]{2,1,0:T(2,128)(2,1)S(1)} %all-to-all-done.1) | data formatting | bytes 1048576
  341.8 8.0 %copy.111 = bf16[1,32,8192]{2,1,0:T(8,128)(2,1)S(1)} copy(bf16[1,32,8192]{1,0,2:T(2,128)(2,1)} %bitcast.120) | data formatting | bytes 1048576 | tf_op jit(solution)/shard_map/all_to_all | solution.py:197
  349.8 0.3 copy.139
  350.1 0.3 copy.112
  350.4 0.9 gather_fusion.1
  351.3 6.0 %convolution_convert_fusion.2 = bf16[128,3200]{1,0:T(8,128)(2,1)} fusion(bf16[3200,1024]{1,0:T(8,128)(2,1)} %param.15, bf16[128,1024]{1,0:T(8,128)(2,1)S(1)} %gather_fusion.1, pred[128]{0:T(512)(128)(4,1)S(1)} %compare_and_fusion.1), kind=kOutput, calls=%fused_computation.12 | convolution fusion | flops 839401472 | bytes 7635072 | tf_op jit(solution)/shard_map/dot_general | solution.py:201
  357.3 2.8 convolution_convert_fusion.4
  360.1 1.0 copy.113
  361.1 50.2 %all-reduce.8.cloned.1.call-done = bf16[128,3200]{1,0:T(8,128)(2,1)} async-done(((bf16[128,3200]{1,0:T(8,128)(2,1)}), bf16[128,3200]{1,0:T(8,128)(2,1)}) %all-reduce.8.cloned.1.call-update) | async-done | bytes 819216 | tf_op jit(solution)/shard_map/psum | solution.py:200
  411.3 1.1 fusion.53
  412.4 11.6 %all-reduce = (f32[16]{0:T(128)S(1)}, f32[16]{0:T(128)S(1)}) all-reduce(f32[16]{0:T(128)S(1)} %get-tuple-element.11, f32[16]{0:T(128)S(1)} %get-tuple-element.10), channel_id=1, replica_groups=mesh['seq'=8,'tp'=4] {'tp'}, use_global_device_ids=true, to_apply=%region_16.17 | all-reduce | flops 32 | bytes 256 | tf_op jit(solution)/shard_map/psum | solution.py:208
  424.0 1.7 fusion.51
  (84 shorter events, 2.5 us)
Async XLA Ops:
  7.2 3.3 copy-start.14
  7.2 5.6 %copy-start.13 = (s32[256]{0:T(256)S(1)}, s32[256]{0:T(256)}, u32[]{:S(2)}) copy-start(s32[256]{0:T(256)} %param.23) | copy-start | bytes 3076
  7.2 5.8 %copy-start.1 = (bf16[16,3200]{1,0:T(8,128)(2,1)S(1)}, bf16[16,3200]{1,0:T(8,128)(2,1)}, u32[]{:S(2)}) copy-start(bf16[16,3200]{1,0:T(8,128)(2,1)} %param.13) | copy-start | bytes 307204
  7.2 18.8 %copy-start.9 = (f32[3200]{0:T(1024)S(1)}, f32[3200]{0:T(1024)}, u32[]{:S(2)}) copy-start(f32[3200]{0:T(1024)} %param.14) | copy-start | bytes 38404
  7.2 140.3 %all-gather.2.cloned.1.call-start = ((), (), s32[]{:S(2)}) async-start(), calls=%async_computation.2 | async-start | bytes 28311552 | tf_op jit(solution)/shard_map/all_gather | solution.py:140
  10.5 70.6 %collective-permute-start.1 = (bf16[256]{0:T(256)(128)(2,1)S(1)}, bf16[256]{0:T(256)(128)(2,1)S(1)}, u32[]{:S(2)}, u32[]{:S(2)}) collective-permute-start(bf16[256]{0:T(256)(128)(2,1)S(1)} %get-tuple-element.19), channel_id=1, source_target_pairs={{0,4},{4,8},{8,12},{12,16},{16,20},{20,24},{24,28},{1,5},{5,9},{9,... | collective-permute-start | bytes 1544 | tf_op jit(solution)/shard_map/ppermute | solution.py:23
  45.2 34.2 %copy-start.12 = (s32[256]{0:T(256)S(1)}, s32[256]{0:T(256)}, u32[]{:S(2)}) copy-start(s32[256]{0:T(256)} %param.22) | copy-start | bytes 3076
  45.2 34.8 %copy-start.2 = (bf16[256,1024]{1,0:T(8,128)(2,1)S(1)}, bf16[256,1024]{1,0:T(8,128)(2,1)}, u32[]{:S(2)}) copy-start(bf16[256,1024]{1,0:T(8,128)(2,1)} %param.25) | copy-start | bytes 1572868
  75.8 19.1 %all-to-all-start = ((bf16[8,32,1024]{2,1,0:T(8,128)(2,1)}), bf16[8,32,1024]{2,1,0:T(8,128)(2,1)S(1)}, u32[]{:S(2)}, u32[]{:S(2)}) async-start(bf16[8,32,1024]{2,1,0:T(8,128)(2,1)} %select_select_fusion), calls=%async_computation | async-start | bytes 1048576 | tf_op jit(solution)/shard_map/all_to_all | solution.py:128
  79.3 186.8 %all-reduce.6.cloned.1.call-start = ((), (), s32[]{:S(2)}) async-start(), calls=%async_computation.3 | async-start | bytes 1048576 | tf_op jit(solution)/shard_map/psum | solution.py:193
  95.0 52.5 %copy-start.10 = (f32[8192]{0:T(1024)S(1)}, f32[8192]{0:T(1024)}, u32[]{:S(2)}) copy-start(f32[8192]{0:T(1024)} %param.17) | copy-start | bytes 98308
  161.9 19.0 %collective-permute-start = (bf16[256,2,128]{0,2,1:T(8,128)(2,1)}, bf16[256,2,128]{0,2,1:T(8,128)(2,1)}, u32[]{:S(2)}, u32[]{:S(2)}) collective-permute-start(bf16[256,2,128]{0,2,1:T(8,128)(2,1)} %bitcast.31), channel_id=1, source_target_pairs={{0,4},{4,8},{8,12},{12,16},{16,20},{20,24},{24,28},{1,5},{5,9},{9,... | collective-permute-start | bytes 393224 | tf_op jit(solution)/shard_map/ppermute | solution.py:23
  166.4 2.9 copy-start.3
  166.4 2.9 copy-start.5
  166.5 3.6 collective-permute-start.2
  170.1 0.6 copy-start.15
  170.8 5.1 %copy-start = (bf16[256,1024]{0,1:T(8,128)(2,1)S(1)}, bf16[256,1024]{0,1:T(8,128)(2,1)}, u32[]{:S(2)}) copy-start(bf16[256,1024]{0,1:T(8,128)(2,1)} %copy.135) | copy-start | bytes 1572868
  178.9 2.0 copy-start.7
  179.6 26.9 %collective-permute-start.4 = (bf16[256,2,128]{0,2,1:T(8,128)(2,1)}, bf16[256,2,128]{0,2,1:T(8,128)(2,1)}, u32[]{:S(2)}, u32[]{:S(2)}) collective-permute-start(bf16[256,2,128]{0,2,1:T(8,128)(2,1)} %slice.98), channel_id=1, source_target_pairs={{4,0},{8,4},{12,8},{16,12},{20,16},{24,20},{28,24},{5,1},{9,5},{13... | collective-permute-start | bytes 393224 | tf_op jit(solution)/shard_map/ppermute | solution.py:23
  184.6 8.3 %copy-start.4 = (bf16[256,2,64]{2,0,1:T(8,128)(2,1)S(1)}, bf16[256,2,64]{2,0,1:T(8,128)(2,1)}, u32[]{:S(2)}) copy-start(bf16[256,2,64]{2,0,1:T(8,128)(2,1)} %copy-done.3) | copy-start | bytes 196612
  184.6 8.3 %copy-start.6 = (bf16[256,2,64]{2,0,1:T(8,128)(2,1)S(1)}, bf16[256,2,64]{2,0,1:T(8,128)(2,1)}, u32[]{:S(2)}) copy-start(bf16[256,2,64]{2,0,1:T(8,128)(2,1)} %copy-done.5) | copy-start | bytes 196612
  184.6 8.3 %copy-start.16 = (bf16[256,2,128]{2,0,1:T(8,128)(2,1)S(1)}, bf16[256,2,128]{2,0,1:T(8,128)(2,1)}, u32[]{:S(2)}) copy-start(bf16[256,2,128]{2,0,1:T(8,128)(2,1)} %copy-done.15) | copy-start | bytes 393220
  202.5 5.5 %collective-permute-start.3 = (bf16[256,2,128]{2,0,1:T(8,128)(2,1)}, bf16[256,2,128]{2,0,1:T(8,128)(2,1)}, u32[]{:S(2)}, u32[]{:S(2)}) collective-permute-start(bf16[256,2,128]{2,0,1:T(8,128)(2,1)} %slice.99), channel_id=1, source_target_pairs={{4,0},{8,4},{12,8},{16,12},{20,16},{24,20},{28,24},{5,1},{9,5},{13... | collective-permute-start | bytes 393224 | tf_op jit(solution)/shard_map/ppermute | solution.py:23
  205.9 1.0 copy-start.8
  209.5 56.6 %copy-start.11 = (f32[8192]{0:T(1024)S(1)}, f32[8192]{0:T(1024)}, u32[]{:S(2)}) copy-start(f32[8192]{0:T(1024)} %param.17) | copy-start | bytes 98308
  276.0 51.9 %copy-start.17 = (s32[128]{0:T(128)S(1)}, s32[128]{0:T(128)}, u32[]{:S(2)}) copy-start(s32[128]{0:T(128)} %param.24) | copy-start | bytes 1540
  323.9 13.4 %all-to-all-start.1 = ((bf16[8,2,16384]{2,1,0:T(2,128)(2,1)}), bf16[8,2,16384]{2,1,0:T(2,128)(2,1)S(1)}, u32[]{:S(2)}, u32[]{:S(2)}) async-start(bf16[8,2,16384]{2,1,0:T(2,128)(2,1)} %reshape.250), calls=%async_computation.1 | async-start | bytes 1048576 | tf_op jit(solution)/shard_map/all_to_all | solution.py:197
  327.6 83.8 %all-reduce.8.cloned.1.call-start = ((), (), s32[]{:S(2)}) async-start(), calls=%async_computation.4 | async-start | bytes 1638400 | tf_op jit(solution)/shard_map/psum | solution.py:200
Sparse Core Ops, SparseCore 0:
  10.6 136.8 all-gather.1
  222.8 43.1 all-reduce.5
  357.4 53.8 all-reduce.7
where the time goes:
time: 433 us; the launch traced here: 432 us
  waiting for transfers between devices  164 us (38%)
  matrix products  70.7 us (16%)
  blocking collectives  67.9 us (16%)
  other arithmetic  60.2 us (14%)
  local copies, waits for them, and re-layouts  37.2 us (9%)
  starting transfers between devices  18.3 us (4%)
  between operations  14.3 us (3%)
    psum x1, waiting for transfers between devices, on_device(): lax.psum(lax.dot_general(token_grads, proj_weight, (((1,), (1,)), ((), ()...  50.2 us
    all_gather x1, waiting for transfers between devices, on_device(): gathered = lax.all_gather(stacked, 'seq', axis=0, tiled=True)  47.7 us
    unnamed x1, other arithmetic  45.2 us
    psum x1, waiting for transfers between devices, on_device(): lax.psum(norm_part.astype(jnp.bfloat16), 'tp').astype(jnp.float32)  43.1 us
    psum x1, blocking collectives, on_device(): summed = lax.psum(partial_embed, 'tp')  28.4 us
    all_gather x1, blocking collectives, on_device(): lax.all_gather(vis_normed, 'seq', axis=0, tiled=True)  15.1 us
    dot_general x1, matrix products, on_device(): lax.dot_general(selected, gathered, (((1,), (1,)), ((), ())), preferred_e...  13.2 us
    all_to_all x1, waiting for transfers between devices, on_device(): lax.all_to_all(outgoing, 'seq', split_axis=0, concat_axis=2, tiled=True)[0]  13 us
  transfers between devices with their start and end apart: 10, of which 6 were waited for; matrix products, arithmetic and copies ran while one was open for 13% of the time, Pallas kernels for 0%

commit v1 on v0

v1 whole, which is shorter than its diff:
```python
import functools
import math

import jax
import jax.numpy as jnp
from jax import lax
from jax.experimental import pallas as pl
from jax.experimental.pallas import tpu as pltpu
from jax.sharding import PartitionSpec as P

VF = 12800
HEAD = 128
CAPD = 32
GROUP = 4


ln_eps = 1e-05
rms_eps = 1e-06
rope_base = 1000000.0
masked_score = -1e30


def shifted(x, axis, by):
    peers = lax.axis_size(axis)
    pairs = [(i, i + by) for i in range(peers) if 0 <= i + by < peers]
    return lax.ppermute(x, axis, pairs)


MESH = pl.DeviceIdType.MESH
VMEM_LIMIT = 56 * 1024 * 1024
NT = (((1,), (1,)), ((), ()))
TN = (((0,), (0,)), ((), ()))
NN = (((1,), (0,)), ((), ()))


def mul(a, b, dims=NN):
    return lax.dot_general(a, b, dims, preferred_element_type=jnp.float32)


def rope_rows(positions):
    half = HEAD // 2
    frequency = rope_base ** (-(jnp.arange(half).astype(jnp.float32) * 2.0 / HEAD))
    angle = positions.astype(jnp.float32)[:, None] * frequency[None, :]
    cosine, sine = jnp.cos(angle), jnp.sin(angle)
    return (
        jnp.concatenate([cosine, cosine], axis=1),
        jnp.concatenate([-sine, sine], axis=1),
    )


def attention_kernel(
    heads, proj_ref, own_ref, prev_ref, cot_ref, qdoc_ref, odoc_ref, pdoc_ref, cos_ref, sin_ref,
    ctx_ref, qg_ref, og_ref, pg_ref, kacc, vacc,
):
    rows = cos_ref.shape[0]
    groups = heads // GROUP
    tail = rows - CAPD
    edge = rows - HEAD
    scale = 1.0 / math.sqrt(HEAD)
    qdoc = qdoc_ref[...]
    near = qdoc == odoc_ref[...]
    row_at = lax.broadcasted_iota(jnp.int32, (rows, rows), 0)
    col_at = lax.broadcasted_iota(jnp.int32, (rows, rows), 1)
    mask1 = near & (col_at <= row_at)
    mask0 = qdoc == pdoc_ref[...]
    for group in range(groups):
        kc = slice(group * HEAD, (group + 1) * HEAD)
        vc = slice((groups + group) * HEAD, (groups + group + 1) * HEAD)
        kp, ko = prev_ref[:, kc], own_ref[:, kc]
        vp, vo = prev_ref[:, vc], own_ref[:, vc]
        kacc[...] = jnp.zeros_like(kacc)
        vacc[...] = jnp.zeros_like(vacc)

        def one_head(member, carry):
            at = pl.multiple_of((group * GROUP + member) * HEAD, HEAD)
            cols = pl.ds(at, HEAD)
            wide = proj_ref[:, cols]
            q = (wide * cos_ref[...] + pltpu.roll(wide, HEAD // 2, 1) * sin_ref[...]).astype(
                jnp.bfloat16
            )
            g = cot_ref[:, cols]
            s0 = jnp.where(mask0, mul(q, kp, NT) * scale, masked_score)
            s1 = jnp.where(mask1, mul(q, ko, NT) * scale, masked_score)
            peak = jnp.maximum(
                jnp.max(s0, axis=1, keepdims=True), jnp.max(s1, axis=1, keepdims=True)
            )
            e0 = jnp.where(mask0, jnp.exp(s0 - peak), 0.0)
            e1 = jnp.where(mask1, jnp.exp(s1 - peak), 0.0)
            total = jnp.sum(e0, axis=1, keepdims=True) + jnp.sum(e1, axis=1, keepdims=True)
            inverse = 1.0 / total
            p0, p1 = e0 * inverse, e1 * inverse
            l0, l1 = p0.astype(jnp.bfloat16), p1.astype(jnp.bfloat16)
            ctx_ref[:, cols] = (mul(l0, vp) + mul(l1, vo)).astype(jnp.bfloat16)
            d0, d1 = mul(g, vp, NT), mul(g, vo, NT)
            delta = jnp.sum(p0 * d0, axis=1, keepdims=True) + jnp.sum(
                p1 * d1, axis=1, keepdims=True
            )
            z0 = (p0 * (d0 - delta) * scale).astype(jnp.bfloat16)
            z1 = (p1 * (d1 - delta) * scale).astype(jnp.bfloat16)
            qg_ref[:, cols] = mul(z0[tail:], kp) + mul(z1[tail:], ko)
            kacc[0] += mul(z0[:, edge:], q, TN)
            kacc[1] += mul(z1[:, edge:], q, TN)
            vacc[0] += mul(l0[:, edge:], g, TN)
            vacc[1] += mul(l1[:, edge:], g, TN)
            return carry

        lax.fori_loop(0, GROUP, one_head, 0)
        pg_ref[:, kc] = kacc[0, HEAD - CAPD :].astype(jnp.bfloat16)
        pg_ref[:, vc] = vacc[0, HEAD - CAPD :].astype(jnp.bfloat16)
        og_ref[:, kc] = kacc[1, HEAD - CAPD :]
        og_ref[:, vc] = vacc[1, HEAD - CAPD :]


def attention(projected, own, prev, cotangent, qdoc, odoc, pdoc, cosine, sine, heads):
    rows = own.shape[0]
    groups = heads // GROUP
    return pl.pallas_call(
        functools.partial(attention_kernel, heads),
        out_shape=(
            jax.ShapeDtypeStruct((rows, heads * HEAD), jnp.bfloat16),
            jax.ShapeDtypeStruct((CAPD, heads * HEAD), jnp.float32),
            jax.ShapeDtypeStruct((CAPD, 2 * groups * HEAD), jnp.float32),
            jax.ShapeDtypeStruct((CAPD, 2 * groups * HEAD), jnp.bfloat16),
        ),
        scratch_shapes=[
            pltpu.VMEM((2, HEAD, HEAD), jnp.float32),
            pltpu.VMEM((2, HEAD, HEAD), jnp.float32),
        ],
        compiler_params=pltpu.CompilerParams(vmem_limit_bytes=VMEM_LIMIT),
    )(projected, own, prev, cotangent, qdoc, odoc, pdoc, cosine, sine)


def exchange(axis, peers, me, source, target, send_sem, recv_sem):
    copies = []
    for step in range(1, peers):
        peer = lax.rem(me + step, peers)
        copies.append(
            pltpu.make_async_remote_copy(
                src_ref=source(peer),
                dst_ref=target(step),
                send_sem=send_sem.at[step - 1],
                recv_sem=recv_sem.at[step - 1],
                device_id={axis: peer},
                device_id_type=MESH,
            )
        )
        copies[-1].start()
    return copies


def both_sums(first, second, lane):
    return jnp.where(
        lane < HEAD // 2,
        jnp.sum(first, axis=1, keepdims=True),
        jnp.sum(second, axis=1, keepdims=True),
    )


def backward_kernel(
    seqs, tps, heads,
    qg_ref, og_ref, pg_ref, cos_ref, sin_ref, pick_ref, route_ref, emb_ref, gain_ref,
    cen_ref, lng_ref, istd_ref, w_hbm, proj_hbm,
    out_ref,
    w_ref, proj_ref, back, pre, gath, part, psend, precv, stat, srecv, eg, fsend, frecv, vstat,
    vrecv, local_sem, back_sem, g_send, g_recv, p_send, p_recv, s_send, s_recv, e_send, e_recv,
    f_send, f_recv, v_send, v_recv,
):
    s, t = lax.axis_index("seq"), lax.axis_index("tp")
    groups = heads // GROUP
    vis = route_ref.shape[0]
    tok = vis // tps
    own_rows = vis // seqs
    width = w_ref.shape[0]
    feats = proj_ref.shape[0]
    load_w = pltpu.make_async_copy(w_hbm, w_ref, local_sem.at[0])
    load_proj = pltpu.make_async_copy(proj_hbm, proj_ref, local_sem.at[1])
    load_w.start()
    load_proj.start()

    barrier = pltpu.get_barrier_semaphore()
    for step in range(1, seqs):
        pl.semaphore_signal(
            barrier, inc=1, device_id={"seq": lax.rem(s + step, seqs)}, device_id_type=MESH
        )
    for step in range(1, tps):
        pl.semaphore_signal(
            barrier, inc=1, device_id={"tp": lax.rem(t + step, tps)}, device_id_type=MESH
        )
    pl.semaphore_wait(barrier, seqs - 1 + tps - 1)

    shift = pltpu.make_async_remote_copy(
        src_ref=pg_ref, dst_ref=back, send_sem=back_sem.at[0], recv_sem=back_sem.at[1],
        device_id={"seq": lax.rem(s + seqs - 1, seqs)}, device_id_type=MESH,
    )
    shift.start()
    cosine, sine = cos_ref[...], sin_ref[...]

    def unrotated(wide):
        return wide * cosine - pltpu.roll(wide, HEAD // 2, 1) * sine

    for head in range(heads):
        cols = slice(head * HEAD, (head + 1) * HEAD)
        pre[:, cols] = unrotated(qg_ref[:, cols]).astype(jnp.bfloat16)
    shift.wait()
    keep = jnp.where(s < seqs - 1, 1.0, 0.0)
    for group in range(2 * groups):
        cols = slice(group * HEAD, (group + 1) * HEAD)
        wide = og_ref[:, cols] + back[:, cols].astype(jnp.float32) * keep
        if group < groups:
            wide = unrotated(wide)
        pre[:, (heads + group) * HEAD : (heads + group + 1) * HEAD] = wide.astype(jnp.bfloat16)
    gath[0] = mul(pick_ref[...], pre[...]).astype(jnp.bfloat16)

    copies = exchange(
        "seq", seqs, s, lambda peer: gath.at[0], lambda step: gath.at[step], g_send, g_recv
    )
    load_w.wait()
    for copy in copies:
        copy.wait()
    slots = gath[...].reshape(seqs * CAPD, gath.shape[2])
    selected = mul(route_ref[...], slots).astype(jnp.bfloat16)
    part[...] = mul(selected, w_ref[...], NT)
    for step in range(1, tps):
        rows = pl.ds(pl.multiple_of(lax.rem(t + step, tps) * tok, 16), tok)
        psend[step - 1] = part[rows, :].astype(jnp.bfloat16)
    copies = []
    for step in range(1, tps):
        copies.append(
            pltpu.make_async_remote_copy(
                src_ref=psend.at[step - 1], dst_ref=precv.at[step - 1],
                send_sem=p_send.at[step - 1], recv_sem=p_recv.at[step - 1],
                device_id={"tp": lax.rem(t + step, tps)}, device_id_type=MESH,
            )
        )
        copies[-1].start()
    mine = pl.ds(pl.multiple_of(t * tok, 16), tok)
    norm_grads = part[mine, :]
    for step, copy in enumerate(copies):
        copy.wait()
        norm_grads += precv[step].astype(jnp.float32)
    emb = emb_ref[mine, :].astype(jnp.float32)
    scaled = norm_grads * gain_ref[...]
    lane = lax.broadcasted_iota(jnp.int32, (tok, HEAD), 1)
    stat[...] = both_sums(emb * emb, emb * scaled, lane)
    copies = exchange(
        "seq", seqs, s, lambda peer: stat, lambda step: srecv.at[step - 1], s_send, s_recv
    )
    sums = stat[...]
    for step, copy in enumerate(copies):
        copy.wait()
        sums += srecv[step]
    inv_rms = lax.rsqrt(sums[:, :1] / (width * seqs) + rms_eps)
    inner = sums[:, HEAD // 2 : HEAD // 2 + 1] / (width * seqs)
    eg[t] = (inv_rms * scaled - emb * (inv_rms * inv_rms * inv_rms) * inner).astype(jnp.bfloat16)
    copies = exchange("tp", tps, t, lambda peer: eg.at[t], lambda step: eg.at[t], e_send, e_recv)
    load_proj.wait()
    for copy in copies:
        copy.wait()
    grads = eg[...].reshape(vis, width)
    chunk = 5 * HEAD
    for begin in range(0, feats, chunk):
        cols = slice(begin, min(begin + chunk, feats))
        block = mul(grads, proj_ref[cols, :], NT)
        fsend[:, :, cols] = block.astype(jnp.bfloat16).reshape(seqs, own_rows, -1)
    copies = exchange(
        "seq", seqs, s, lambda peer: fsend.at[peer], lambda step: frecv.at[step - 1], f_send,
        f_recv,
    )
    total = fsend[s].astype(jnp.float32)
    for step, copy in enumerate(copies):
        copy.wait()
        total += frecv[step].astype(jnp.float32)
    centred = cen_ref[...]
    scaled = total * lng_ref[...]
    lane = lax.broadcasted_iota(jnp.int32, (own_rows, HEAD), 1)
    vstat[...] = both_sums(scaled, scaled * centred, lane)
    copies = exchange(
        "tp", tps, t, lambda peer: vstat, lambda step: vrecv.at[step - 1], v_send, v_recv
    )
    sums = vstat[...]
    for step, copy in enumerate(copies):
        copy.wait()
        sums += vrecv[step]
    mean = sums[:, :1] / VF
    inner = sums[:, HEAD // 2 : HEAD // 2 + 1] / VF
    out_ref[...] = (istd_ref[...] * (scaled - mean - centred * inner)).astype(jnp.bfloat16)


def backward(qg, og, pg, cosine, sine, pick, route, emb, gain, centred, lng, istd, w, proj, heads):
    seqs, tps = lax.axis_size("seq"), lax.axis_size("tp")
    vis = route.shape[0]
    tok, own_rows = vis // tps, vis // seqs
    width, cols = w.shape
    feats = proj.shape[0]
    bf, f32 = jnp.bfloat16, jnp.float32
    sem = pltpu.SemaphoreType.DMA
    vm = pl.BlockSpec(memory_space=pltpu.VMEM)
    hb = pl.BlockSpec(memory_space=pl.ANY)
    return pl.pallas_call(
        functools.partial(backward_kernel, seqs, tps, heads),
        out_shape=jax.ShapeDtypeStruct((own_rows, feats), bf),
        in_specs=[vm] * 12 + [hb] * 2,
        out_specs=vm,
        scratch_shapes=[
            pltpu.VMEM((width, cols), bf),
            pltpu.VMEM((feats, width), bf),
            pltpu.VMEM(pg.shape, bf),
            pltpu.VMEM((CAPD, cols), bf),
            pltpu.VMEM((seqs, CAPD, cols), bf),
            pltpu.VMEM((vis, width), f32),
            pltpu.VMEM((tps - 1, tok, width), bf),
            pltpu.VMEM((tps - 1, tok, width), bf),
            pltpu.VMEM((tok, HEAD), f32),
            pltpu.VMEM((seqs - 1, tok, HEAD), f32),
            pltpu.VMEM((tps, tok, width), bf),
            pltpu.VMEM((seqs, own_rows, feats), bf),
            pltpu.VMEM((seqs - 1, own_rows, feats), bf),
            pltpu.VMEM((own_rows, HEAD), f32),
            pltpu.VMEM((tps - 1, own_rows, HEAD), f32),
            sem((2,)),
            sem((2,)),
            sem((seqs - 1,)),
            sem((seqs - 1,)),
            sem((tps - 1,)),
            sem((tps - 1,)),
            sem((seqs - 1,)),
            sem((seqs - 1,)),
            sem((tps - 1,)),
            sem((tps - 1,)),
            sem((seqs - 1,)),
            sem((seqs - 1,)),
            sem((tps - 1,)),
            sem((tps - 1,)),
        ],
        compiler_params=pltpu.CompilerParams(
            collective_id=0, has_side_effects=True, vmem_limit_bytes=VMEM_LIMIT
        ),
    )(qg, og, pg, cosine, sine, pick, route, emb, gain, centred, lng, istd, w, proj)


def on_device(
    vis_feat,
    ln_gain,
    proj_weight,
    text_embed,
    rms_gain,
    wq,
    wk,
    wv,
    doc_ids,
    vis_slot,
    slot_token,
    token_slot,
    cotangent,
):
    seq_count = lax.axis_size("seq")
    my_index = lax.axis_index("seq")
    tok_rows = text_embed.shape[0]
    slot_cols = proj_weight.shape[1]
    features = vis_feat.astype(jnp.float32)
    row_total, row_squares = lax.psum(
        (jnp.sum(features, axis=1), jnp.sum(features * features, axis=1)), "tp"
    )
    row_mean = row_total / VF
    row_var = row_squares / VF - row_mean * row_mean
    inv_std = lax.rsqrt(row_var + ln_eps)
    centred = (features - row_mean[:, None]) * inv_std[:, None]
    vis_normed = (centred * ln_gain[None, :]).astype(jnp.bfloat16)
    partial_embed = jnp.dot(
        lax.all_gather(vis_normed, "seq", axis=0, tiled=True),
        proj_weight,
        preferred_element_type=jnp.float32,
    )
    slot_live = (slot_token >= 0)[:, None]
    slot_index = jnp.maximum(slot_token, 0)
    summed = lax.psum(partial_embed, "tp")
    embed = summed.astype(jnp.bfloat16)
    embed_rows = jnp.take(embed, slot_index, axis=0)
    outgoing = jnp.where(slot_live, embed_rows, jnp.zeros_like(embed_rows)).reshape(
        seq_count, CAPD, slot_cols
    )
    arrived = lax.all_to_all(outgoing, "seq", split_axis=0, concat_axis=2, tiled=True)[0]
    lanes = jnp.arange(CAPD, dtype=jnp.int32)
    one_hot = (vis_slot[:, None] == lanes[None, :]).astype(jnp.bfloat16)
    placed = jnp.dot(one_hot, arrived, preferred_element_type=jnp.float32).astype(jnp.bfloat16)
    is_image = vis_slot >= 0
    hidden = jnp.where(is_image[:, None], placed, text_embed)
    hidden_wide = hidden.astype(jnp.float32)
    inv_rms = lax.rsqrt(jnp.mean(hidden_wide * hidden_wide, axis=1, keepdims=True) + rms_eps)
    normed = (hidden_wide * inv_rms * rms_gain[None, :]).astype(jnp.bfloat16)
    stacked = jnp.concatenate([wq, wk, wv], axis=1)
    query_cols = wq.shape[1]
    key_cols = wk.shape[1]
    gathered = lax.all_gather(stacked, "seq", axis=0, tiled=True)
    projected = jnp.dot(normed, gathered, preferred_element_type=jnp.float32)
    heads = query_cols // HEAD
    groups = key_cols // HEAD
    positions = my_index * tok_rows + jnp.arange(tok_rows, dtype=jnp.int32)
    cosine, sine = rope_rows(positions)
    pieces = []
    for group in range(groups):
        wide = projected[:, query_cols + group * HEAD : query_cols + (group + 1) * HEAD]
        turned = jnp.concatenate([wide[:, HEAD // 2 :], wide[:, : HEAD // 2]], axis=1)
        pieces.append((wide * cosine + turned * sine).astype(jnp.bfloat16))
    pieces.append(projected[:, query_cols + key_cols :].astype(jnp.bfloat16))
    own = jnp.concatenate(pieces, axis=1)
    doc_marks = (doc_ids + 1).astype(jnp.bfloat16)
    prev_docs = shifted(doc_marks, "seq", 1)
    prev = shifted(own, "seq", 1)
    query_docs = doc_marks.astype(jnp.float32)
    context, query_grads, own_grads, prev_grads = attention(
        projected,
        own,
        prev,
        cotangent,
        query_docs[:, None],
        query_docs[None, :],
        prev_docs.astype(jnp.float32)[None, :],
        cosine,
        sine,
        heads,
    )
    tail = tok_rows - CAPD
    pick = (lanes[:, None] == vis_slot[None, tail:]).astype(jnp.bfloat16)
    slot_ids = jnp.arange(seq_count * CAPD, dtype=jnp.int32)
    source = (my_index - slot_ids // CAPD + seq_count) % seq_count
    held = source * CAPD + slot_ids % CAPD
    route = (token_slot[:, None] == held[None, :]).astype(jnp.bfloat16)
    gain = lax.dynamic_slice_in_dim(rms_gain, my_index * slot_cols, slot_cols, 0)
    vis_grad = backward(
        query_grads,
        own_grads,
        prev_grads,
        cosine[tail:],
        sine[tail:],
        pick,
        route,
        embed,
        gain[None, :],
        centred,
        ln_gain[None, :],
        inv_std[:, None],
        stacked,
        proj_weight,
        heads,
    )
    return (context, vis_grad)


def solution(mesh):
    return jax.shard_map(
        on_device,
        mesh=mesh,
        in_specs=(
            P("seq", "tp"),
            P("tp"),
            P("tp", "seq"),
            P("seq", None),
            P(),
            P("seq", "tp"),
            P("seq", "tp"),
            P("seq", "tp"),
            P("seq"),
            P("seq"),
            P(),
            P(),
            P("seq", "tp"),
        ),
        out_specs=(P("seq", "tp"), P("seq", "tp")),
        check_vma=False,
    )
```

time: 433 us -> 243 us (0.56)
  waiting for transfers between devices: 164 us -> 59.4 us
  Pallas kernels: 0 us -> 65.3 us
  other arithmetic: 60.2 us -> 6.25 us
  matrix products: 70.7 us -> 22 us
  local copies, waits for them, and re-layouts: 37.2 us -> 10.1 us
  blocking collectives: 67.9 us -> 56.8 us
  starting transfers between devices: 18.3 us -> 8.18 us
    psum x2 -> x0, waiting for transfers between devices: 93.3 us -> none  [the longest x1 50.2 us: on_device(): lax.psum(lax.dot_general(token_grads, proj_weight, (((1,), (1,)), ((), ()...]
    pallas_call x0 -> x2, Pallas kernels: none -> 65.3 us  [the longest x1 54.4 us: backward(): pl.pallas_call(functools.partial(backward_kernel, seqs, tps, heads), out_...]
    unnamed x1 -> x0, other arithmetic: 45.2 us -> none
    dot_general x7 -> x0, matrix products: 43.9 us -> none  [the longest x1 13.2 us: on_device(): lax.dot_general(selected, gathered, (((1,), (1,)), ((), ())), preferred_e...]
    psum x1 -> x0, blocking collectives: 11.6 us -> none  [on_device(): lax.psum((jnp.sum(scaled, axis=1), jnp.sum(scaled * centred, axis=1)), 'tp')]
    all_to_all x1 -> x0, waiting for transfers between devices: 9.39 us -> none  [on_device(): lax.all_to_all(embed_grads[None], 'seq', split_axis=2, concat_axis=0, til...]
    all_to_all x3 -> x0, local copies, waits for them, and re-layouts: 8.3 us -> none  [on_device(): lax.all_to_all(embed_grads[None], 'seq', split_axis=2, concat_axis=0, til...]
    unnamed x47 -> x36, local copies, waits for them, and re-layouts: 12.3 us -> 5.84 us
  transfers between devices with their start and end apart: 10 -> 4, of which waited for: 6 -> 2; matrix products, arithmetic and copies ran while one was open for 13% -> 13% of each run, Pallas kernels for 0% -> 0%
where the time goes in v1:
time: 243 us; the launch traced here: 242 us
  Pallas kernels  65.3 us (27%)
  waiting for transfers between devices  59.4 us (24%)
  blocking collectives  56.8 us (23%)
  matrix products  22 us (9%)
  between operations  14.4 us (6%)
  local copies, waits for them, and re-layouts  10.1 us (4%)
  starting transfers between devices  8.18 us (3%)
  other arithmetic  6.25 us (3%)
    pallas_call x1, Pallas kernels, backward(): pl.pallas_call(functools.partial(backward_kernel, seqs, tps, heads), out_...  54.4 us
    all_gather x1, waiting for transfers between devices, on_device(): gathered = lax.all_gather(stacked, 'seq', axis=0, tiled=True)  48 us
    psum x1, blocking collectives, on_device(): summed = lax.psum(partial_embed, 'tp')  28.3 us
    all_gather x1, blocking collectives, on_device(): lax.all_gather(vis_normed, 'seq', axis=0, tiled=True)  15.1 us
    psum x1, blocking collectives, on_device(): lax.psum((jnp.sum(features, axis=1), jnp.sum(features * features, axis=1)...  13.5 us
    dot_general x1, matrix products, on_device(): projected = jnp.dot(normed, gathered, preferred_element_type=jnp.float32)  12.8 us
    all_to_all x1, waiting for transfers between devices, on_device(): lax.all_to_all(outgoing, 'seq', split_axis=0, concat_axis=2, tiled=True)[0]  11.3 us
    pallas_call x1, Pallas kernels, attention(): pl.pallas_call(functools.partial(attention_kernel, heads), out_shape=(jax...  10.9 us
  transfers between devices with their start and end apart: 4, of which 2 were waited for; matrix products, arithmetic and copies ran while one was open for 13% of the time, Pallas kernels for 0%

profile of v1, /device:TPU:0, one launch (start us, length us, event | category | flops | bytes accessed | tf_op | source)
XLA Modules:
  0.0 242.3 jit_solution(14788831487220507075)
XLA Ops:
  7.2 0.0 copy-start.7
  7.2 0.0 copy-start.9
  7.2 0.0 all-gather.2.cloned.1.call-start
  7.2 0.0 copy-start.5
  7.2 0.0 copy-start.6
  7.2 1.8 constant_dynamic-update-slice_fusion.2
  9.1 0.0 copy-done.5
  9.2 0.0 copy-done.6
  9.2 0.0 copy-start.1
  9.2 1.6 copy-done.1
  10.8 0.0 all-gather.2.cloned.1.call-update
  10.9 0.0 copy-done.7
  10.9 0.1 convert_reduce_fusion
  11.0 13.5 %all-reduce = (f32[16]{0:T(128)S(1)}, f32[16]{0:T(128)S(1)}) all-reduce(f32[16]{0:T(128)S(1)} %get-tuple-element.11, f32[16]{0:T(128)S(1)} %get-tuple-element.10), channel_id=1, replica_groups=mesh['seq'=8,'tp'=4] {'tp'}, use_global_device_ids=true, to_apply=%region_3.0 | all-reduce | flops 32 | bytes 256 | tf_op jit(solution)/shard_map/psum | solution.py:361
  24.5 0.0 copy-done.9
  24.5 0.8 fusion.8
  25.3 15.1 %all_gather.6 = bf16[128,3200]{1,0:T(8,128)(2,1)S(1)} all-gather(bf16[16,3200]{1,0:T(8,128)(2,1)S(1)} %get-tuple-element.24), channel_id=1, replica_groups=mesh['seq'=8,'tp'=4] {'seq'}, dimensions={0}, use_global_device_ids=true | all-gather | bytes 921600 | tf_op jit(solution)/shard_map/all_gather | solution.py:370
  40.3 4.0 %fusion.28 = f32[128,1024]{1,0:T(8,128)S(1)} fusion(bf16[128,3200]{1,0:T(8,128)(2,1)S(1)} %all_gather.6, bf16[3200,1024]{1,0:T(8,128)(2,1)} %proj_hbm.1), kind=kOutput, calls=%fused_computation.75 | convolution fusion | flops 838860800 | bytes 7897088 | tf_op jit(solution)/shard_map/dot_general | solution.py:369
  44.3 0.0 copy-done.11
  44.3 0.0 copy-start.12
  44.4 0.1 broadcast_in_dim.71
  44.4 0.1 broadcast_in_dim.73
  44.5 0.0 copy-start.15
  44.6 28.3 %all-reduce.2.emb_ref = bf16[128,1024]{1,0:T(8,128)(2,1)S(1)} all-reduce(f32[128,1024]{1,0:T(8,128)S(1)} %fusion.28), channel_id=1, replica_groups=mesh['seq'=8,'tp'=4] {'tp'}, use_global_device_ids=true, to_apply=%region_4.0 | all-reduce | flops 131072 | bytes 786432 | tf_op jit(solution)/shard_map/psum | solution.py:376
  72.9 0.0 copy-start
  72.9 1.2 gather_fusion
  74.0 0.9 select_select_fusion
  75.0 3.5 %all-to-all-start = ((bf16[8,32,1024]{2,1,0:T(8,128)(2,1)}), bf16[8,32,1024]{2,1,0:T(8,128)(2,1)S(1)}, u32[]{:S(2)}, u32[]{:S(2)}) async-start(bf16[8,32,1024]{2,1,0:T(8,128)(2,1)} %select_select_fusion), calls=%async_computation | async-start | bytes 1048576 | tf_op jit(solution)/shard_map/all_to_all | solution.py:382
  78.5 0.0 copy-done.12
  78.5 0.0 copy-start.10
  78.5 2.3 collective-permute-start.1
  80.9 0.5 fusion.15
  81.4 0.7 fusion.16
  82.1 0.0 copy-done.15
  82.1 0.1 slice.44
  82.2 0.6 fusion.18.pick_ref
  82.8 11.3 %all-to-all-done = bf16[8,32,1024]{2,1,0:T(8,128)(2,1)S(1)} async-done(((bf16[8,32,1024]{2,1,0:T(8,128)(2,1)}), bf16[8,32,1024]{2,1,0:T(8,128)(2,1)S(1)}, u32[]{:S(2)}, u32[]{:S(2)}) %all-to-all-start) | async-done | bytes 524320 | tf_op jit(solution)/shard_map/all_to_all | solution.py:382
  94.1 0.0 copy-done
  94.2 0.0 copy-start.14
  94.2 5.2 %fusion.1 = (f32[256]{0:T(256)S(1)}, bf16[256,8192]{1,0:T(8,128)(2,1)}) fusion(bf16[256,8192]{1,0:T(8,128)(2,1)} %param.16, bf16[32,8192]{1,0:T(8,128)(2,1)S(1)} %bitcast.20, s32[256]{0:T(256)S(1)} %copy-done.15, pred[256]{0:T(512)(128)(4,1)S(1)} %broadcast_compare_fusion.2), kind=kOutput, calls=%fused_computation.5 | convolution fusion | flops 144711424 | bytes 8915200 | tf_op jit(solution)/shard_map/dot_general | solution.py:385
  99.3 48.0 %all-gather.2.cloned.1.call-done = bf16[8192,1536]{1,0:T(8,128)(2,1)} async-done(((bf16[1024,1536]{1,0:T(8,128)(2,1)}), bf16[8192,1536]{1,0:T(8,128)(2,1)}) %all-gather.2.cloned.1.call-update) | async-done | bytes 25165840 | tf_op jit(solution)/shard_map/all_gather | solution.py:394
  147.3 0.0 copy-done.14
  147.3 12.8 %fusion.4.proj_ref = f32[256,1536]{1,0:T(8,128)S(1)} fusion(bf16[8192,1536]{1,0:T(8,128)(2,1)} %all-gather.2.cloned.1.call-done, bf16[256,8192]{1,0:T(8,128)(2,1)} %get-tuple-element.33, f32[8192]{0:T(1024)S(1)} %copy-done.14, f32[256]{0:T(256)S(1)} %add_rsqrt_fusion), kind=kOutput, calls=%fused_computation.8 | convolution fusion | flops 6450839552 | bytes 30966784 | tf_op jit(solution)/shard_map/dot_general | solution.py:395
  160.2 0.0 copy-start.2
  160.2 0.1 fusion.27
  160.4 1.0 fusion.13
  161.4 0.1 fusion.11
  161.6 0.0 copy-start.4
  161.6 2.4 collective-permute-start
  164.0 0.6 broadcast_in_dim.83.lng_ref
  164.6 0.0 copy-done.10
  164.6 0.8 copy.25.qdoc_ref
  165.4 0.7 compare_convert_fusion.route_ref
  166.1 0.6 dynamic_slice.3
  166.7 0.7 copy.26.istd_ref
  167.4 0.0 collective-permute-done.1
  167.4 0.6 broadcast_in_dim.85
  168.0 0.0 collective-permute-done.prev_ref
  168.0 0.0 copy-done.3
  168.0 0.0 copy-done.4
  168.0 0.7 copy-done.8
  168.7 10.9 %shard_map.140 = (bf16[256,1024]{1,0:T(8,128)(2,1)}, f32[32,1024]{1,0:T(8,128)}, f32[32,512]{1,0:T(8,128)}, bf16[32,512]{1,0:T(8,128)(2,1)}) custom-call(f32[256,1536]{1,0:T(8,128)} %copy-done.2, bf16[256,512]{1,0:T(8,128)(2,1)} %copy-done.4, bf16[256,512]{1,0:T(8,128)(2,1)} %copy-done.8, bf16[256,1024]{1,0:T(8,128)(2,1)} %cot_ref.1, ...), custom_call_target="tpu_custom_call" | custom-call | tf_op jit(solution)/shard_map/pallas_call | solution.py:117
  179.6 54.4 %shard_map.141 = bf16[16,3200]{1,0:T(8,128)(2,1)} custom-call(f32[32,1024]{1,0:T(8,128)} %get-tuple-element.7.qg_ref, f32[32,512]{1,0:T(8,128)} %get-tuple-element.8.og_ref, bf16[32,512]{1,0:T(8,128)(2,1)} %get-tuple-element.9.pg_ref, f32[32,128]{1,0:T(8,128)} %get-tuple-element.35.cos_ref, f32[32,128]{1,0:T(8,128)} %get-tuple-element.34.sin_ref, ...), custom_call_target="tpu_custom_call" | custom-call | tf_op jit(solution)/shard_map/pallas_call | solution.py:299
  234.0 1.5 copy.34
  (21 shorter events, 0.2 us)
Async XLA Ops:
  7.2 3.7 %copy-start.7 = (bf16[16,3200]{1,0:T(8,128)(2,1)S(1)}, bf16[16,3200]{1,0:T(8,128)(2,1)}, u32[]{:S(2)}) copy-start(bf16[16,3200]{1,0:T(8,128)(2,1)} %param.13) | copy-start | bytes 307204
  7.2 17.3 %copy-start.9 = (f32[3200]{0:T(1024)S(1)}, f32[3200]{0:T(1024)}, u32[]{:S(2)}) copy-start(f32[3200]{0:T(1024)} %param.14) | copy-start | bytes 38404
  7.2 140.1 %all-gather.2.cloned.1.call-start = ((), (), s32[]{:S(2)}) async-start(), calls=%async_computation.1 | async-start | bytes 28311552 | tf_op jit(solution)/shard_map/all_gather | solution.py:394
  7.2 1.9 copy-start.5
  7.2 1.9 copy-start.6
  9.2 1.6 copy-start.1
  25.3 19.1 %copy-start.11 = (s32[256]{0:T(256)S(1)}, s32[256]{0:T(256)}, u32[]{:S(2)}) copy-start(s32[256]{0:T(256)} %param.23) | copy-start | bytes 3076
  44.3 34.2 %copy-start.12 = (s32[256]{0:T(256)S(1)}, s32[256]{0:T(256)}, u32[]{:S(2)}) copy-start(s32[256]{0:T(256)} %param.21) | copy-start | bytes 3076
  44.5 37.5 %copy-start.15 = (s32[256]{0:T(256)S(1)}, s32[256]{0:T(256)}, u32[]{:S(2)}) copy-start(s32[256]{0:T(256)} %param.22) | copy-start | bytes 3076
  72.9 21.3 %copy-start = (bf16[128,1024]{1,0:T(8,128)(2,1)}, bf16[128,1024]{1,0:T(8,128)(2,1)S(1)}, u32[]{:S(2)}) copy-start(bf16[128,1024]{1,0:T(8,128)(2,1)S(1)} %all-reduce.2.emb_ref) | copy-start | bytes 786436
  75.0 19.1 %all-to-all-start = ((bf16[8,32,1024]{2,1,0:T(8,128)(2,1)}), bf16[8,32,1024]{2,1,0:T(8,128)(2,1)S(1)}, u32[]{:S(2)}, u32[]{:S(2)}) async-start(bf16[8,32,1024]{2,1,0:T(8,128)(2,1)} %select_select_fusion), calls=%async_computation | async-start | bytes 1048576 | tf_op jit(solution)/shard_map/all_to_all | solution.py:382
  78.5 86.1 %copy-start.10 = (f32[256]{0:T(256)}, f32[256]{0:T(256)S(1)}, u32[]{:S(2)}) copy-start(f32[256]{0:T(256)S(1)} %get-tuple-element.14) | copy-start | bytes 3076
  78.5 88.8 %collective-permute-start.1 = (bf16[256]{0:T(256)(128)(2,1)S(1)}, bf16[256]{0:T(256)(128)(2,1)S(1)}, u32[]{:S(2)}, u32[]{:S(2)}) collective-permute-start(bf16[256]{0:T(256)(128)(2,1)S(1)} %get-tuple-element.15), channel_id=1, source_target_pairs={{0,4},{4,8},{8,12},{12,16},{16,20},{20,24},{24,28},{1,5},{5,9},{9,... | collective-permute-start | bytes 1544 | tf_op jit(solution)/shard_map/ppermute | solution.py:26
  94.2 53.2 %copy-start.14 = (f32[8192]{0:T(1024)S(1)}, f32[8192]{0:T(1024)}, u32[]{:S(2)}) copy-start(f32[8192]{0:T(1024)} %param.17) | copy-start | bytes 98308
  147.3 18.1 %copy-start.13 = (s32[128]{0:T(128)S(1)}, s32[128]{0:T(128)}, u32[]{:S(2)}) copy-start(s32[128]{0:T(128)} %param.24) | copy-start | bytes 1540
  160.2 7.8 %copy-start.2 = (f32[256,1536]{1,0:T(8,128)}, f32[256,1536]{1,0:T(8,128)S(1)}, u32[]{:S(2)}) copy-start(f32[256,1536]{1,0:T(8,128)S(1)} %fusion.4.proj_ref) | copy-start | bytes 4718596
  161.4 6.6 %copy-start.3 = (f32[256,128]{1,0:T(8,128)}, f32[256,128]{1,0:T(8,128)S(1)}, u32[]{:S(2)}) copy-start(f32[256,128]{1,0:T(8,128)S(1)} %get-tuple-element.17.sin_ref) | copy-start | bytes 393220
  161.6 6.4 %copy-start.4 = (bf16[256,512]{1,0:T(8,128)(2,1)}, bf16[256,512]{1,0:T(8,128)(2,1)S(1)}, u32[]{:S(2)}) copy-start(bf16[256,512]{1,0:T(8,128)(2,1)S(1)} %pad_maximum_fusion.own_ref) | copy-start | bytes 786436
  161.6 6.4 %collective-permute-start = (bf16[256,512]{1,0:T(8,128)(2,1)S(1)}, bf16[256,512]{1,0:T(8,128)(2,1)S(1)}, u32[]{:S(2)}, u32[]{:S(2)}) collective-permute-start(bf16[256,512]{1,0:T(8,128)(2,1)S(1)} %pad_maximum_fusion.own_ref), channel_id=1, source_target_pairs={{0,4},{4,8},{8,12},{12,16},{16,20},{20,24},{24,28},{1,5},{5,9},{9,... | collective-permute-start | bytes 786440 | tf_op jit(solution)/shard_map/ppermute | solution.py:26
  168.0 0.7 copy-start.8
Sparse Core Ops, SparseCore 0:
  11.0 136.2 all-gather.1

commit v2 on v1

--- a/solution.py
+++ b/solution.py
@@ -156,10 +156,279 @@
     )
 
 
+def weight_loads(sources, target, sems):
+    loads, at = [], 0
+    for index, source in enumerate(sources):
+        wide = source.shape[1]
+        loads.append(
+            pltpu.make_async_copy(source, target.at[:, at : at + wide], sems.at[index])
+        )
+        at += wide
+    return loads
+
+
+def greet(seqs, tps, s, t):
+    barrier = pltpu.get_barrier_semaphore()
+    for step in range(1, seqs):
+        pl.semaphore_signal(
+            barrier, inc=1, device_id={"seq": lax.rem(s + step, seqs)}, device_id_type=MESH
+        )
+    for step in range(1, tps):
+        pl.semaphore_signal(
+            barrier, inc=1, device_id={"tp": lax.rem(t + step, tps)}, device_id_type=MESH
+        )
+    pl.semaphore_wait(barrier, seqs - 1 + tps - 1)
+
+
+def forward_kernel(
+    seqs, tps, heads,
+    feat_ref, lng_ref, route_ref, place_ref, image_ref, rgain_ref, cos_ref, sin_ref,
+    wq_hbm, wk_hbm, wv_hbm, proj_hbm, text_hbm,
+    query_ref, own_ref, prev_ref, emb_ref, cen_ref, istd_ref,
+    gw, proj_ref, hid, acc, nrm, stat, vrecv, part, precv, emb_s, out_s, arr, kvs, kvr,
+    local_sem, w_send, w_recv, v_send, v_recv, n_send, n_recv, p_send, p_recv, e_send, e_recv,
+    a_send, a_recv, k_sem,
+):
+    s, t = lax.axis_index("seq"), lax.axis_index("tp")
+    groups = heads // GROUP
+    own_rows, feats = feat_ref.shape
+    width = gw.shape[1]
+    vis = own_rows * seqs
+    tok = vis // tps
+    rows = hid.shape[0]
+    tail = rows - CAPD
+    loads = weight_loads((wq_hbm, wk_hbm, wv_hbm), gw.at[s], local_sem)
+    load_proj = pltpu.make_async_copy(proj_hbm, proj_ref, local_sem.at[3])
+    load_text = pltpu.make_async_copy(text_hbm, hid, local_sem.at[4])
+    for load in loads:
+        load.start()
+    load_proj.start()
+    load_text.start()
+    greet(seqs, tps, s, t)
+    for load in loads:
+        load.wait()
+
+    def other(bits):
+        low, mid, high = s % 2, (s // 2) % 2, s // 4
+        low = 1 - low if bits & 1 else low
+        mid = 1 - mid if bits & 2 else mid
+        high = 1 - high if bits & 4 else high
+        return high * 4 + mid * 2 + low
+
+    half = width // 2
+    parts = (pl.ds(0, half), pl.ds(half, half))
+
+    def send(number, owner, piece, bits):
+        where = gw.at[owner] if piece is None else gw.at[owner, parts[piece]]
+        copy = pltpu.make_async_remote_copy(
+            src_ref=where, dst_ref=where,
+            send_sem=w_send.at[number], recv_sem=w_recv.at[number],
+            device_id={"seq": other(bits)}, device_id_type=MESH,
+        )
+        copy.start()
+        return copy
+
+    grid = seqs == 8
+    if grid:
+        x_a = send(0, s, 0, 2)
+        y_b = send(1, s, 1, 4)
+        x_b = send(2, s, 1, 2)
+        y_a = send(3, s, 0, 4)
+        core = send(4, s, None, 1)
+    else:
+        spread = exchange(
+            "seq", seqs, s, lambda peer: gw.at[s], lambda step: gw.at[s], w_send, w_recv
+        )
+
+    features = feat_ref[...].astype(jnp.float32)
+    lane = lax.broadcasted_iota(jnp.int32, (own_rows, HEAD), 1)
+    stat[...] = both_sums(features, features * features, lane)
+    copies = exchange(
+        "tp", tps, t, lambda peer: stat, lambda step: vrecv.at[step - 1], v_send, v_recv
+    )
+    sums = stat[...]
+    for step, copy in enumerate(copies):
+        copy.wait()
+        sums += vrecv[step]
+    mean = sums[:, :1] / VF
+    var = sums[:, HEAD // 2 : HEAD // 2 + 1] / VF - mean * mean
+    inv_std = lax.rsqrt(var + ln_eps)
+    centred = (features - mean) * inv_std
+    cen_ref[...] = centred
+    istd_ref[...] = jnp.broadcast_to(inv_std, istd_ref.shape)
+    nrm[s] = (centred * lng_ref[...]).astype(jnp.bfloat16)
+    copies = exchange("seq", seqs, s, lambda peer: nrm.at[s], lambda step: nrm.at[s], n_send, n_recv)
+    load_proj.wait()
+    for copy in copies:
+        copy.wait()
+    part[...] = mul(nrm[...].reshape(vis, feats), proj_ref[...])
+    copies = []
+    for step in range(1, tps):
+        peer = lax.rem(t + step, tps)
+        copies.append(
+            pltpu.make_async_remote_copy(
+                src_ref=part.at[pl.ds(pl.multiple_of(peer * tok, 16), tok)],
+                dst_ref=precv.at[step - 1],
+                send_sem=p_send.at[step - 1], recv_sem=p_recv.at[step - 1],
+                device_id={"tp": peer}, device_id_type=MESH,
+            )
+        )
+        copies[-1].start()
+    total = part[pl.ds(pl.multiple_of(t * tok, 16), tok), :]
+    for step, copy in enumerate(copies):
+        copy.wait()
+        total += precv[step]
+    emb_s[t] = total.astype(jnp.bfloat16)
+    copies = exchange(
+        "tp", tps, t, lambda peer: emb_s.at[t], lambda step: emb_s.at[t], e_send, e_recv
+    )
+    load_text.wait()
+    for copy in copies:
+        copy.wait()
+    embed = emb_s[...].reshape(vis, width)
+    emb_ref[...] = embed
+    out_s[...] = mul(route_ref[...], embed).astype(jnp.bfloat16).reshape(seqs, CAPD, width)
+    arr[s] = out_s[s]
+    copies = exchange(
+        "seq", seqs, s, lambda peer: out_s.at[peer], lambda step: arr.at[s], a_send, a_recv
+    )
+    if grid:
+        x_a.wait()
+        turn_y = send(5, other(2), 0, 4)
+        y_b.wait()
+        turn_x = send(6, other(4), 1, 2)
+    for copy in copies:
+        copy.wait()
+    image = image_ref[...] > 0.0
+    square = jnp.zeros((rows, 1), jnp.float32)
+    for index in range(seqs):
+        cols = slice(index * width, (index + 1) * width)
+        placed = mul(place_ref[...], arr[index])
+        text = hid[tail:, cols].astype(jnp.float32)
+        hid[tail:, cols] = jnp.where(image, placed, text).astype(jnp.bfloat16)
+        wide = hid[:, cols].astype(jnp.float32)
+        square += jnp.sum(wide * wide, axis=1, keepdims=True)
+    inv_rms = lax.rsqrt(square / (width * seqs) + rms_eps)
+
+    def project(owner):
+        cols = pl.ds(pl.multiple_of(owner * width, HEAD), width)
+        wide = hid[:, cols].astype(jnp.float32)
+        normed = (wide * inv_rms * rgain_ref[:, cols]).astype(jnp.bfloat16)
+        return mul(normed, gw[owner])
+
+    acc[...] = project(s)
+    if grid:
+        core.wait()
+        x_b.wait()
+        core_x = send(7, other(2), None, 1)
+        y_a.wait()
+        core_y = send(8, other(4), None, 1)
+        acc[...] += project(other(1))
+        acc[...] += project(other(2))
+        acc[...] += project(other(4))
+        core_x.wait()
+        acc[...] += project(other(3))
+        core_y.wait()
+        acc[...] += project(other(5))
+        turn_y.wait()
+        core_a = send(9, other(6), 0, 1)
+        turn_x.wait()
+        core_b = send(10, other(6), 1, 1)
+        acc[...] += project(other(6))
+        core_a.wait()
+        core_b.wait()
+        acc[...] += project(other(7))
+    else:
+        for step, copy in enumerate(spread):
+            copy.wait()
+            acc[...] += project(lax.rem(s - step - 1 + seqs, seqs))
+    key_at = heads * HEAD
+    cosine, sine = cos_ref[...], sin_ref[...]
+    for group in range(2 * groups):
+        cols = slice(group * HEAD, (group + 1) * HEAD)
+        wide = acc[:, key_at + group * HEAD : key_at + (group + 1) * HEAD]
+        if group < groups:
+            wide = wide * cosine + pltpu.roll(wide, HEAD // 2, 1) * sine
+        kvs[:, cols] = wide.astype(jnp.bfloat16)
+    shift = pltpu.make_async_remote_copy(
+        src_ref=kvs, dst_ref=kvr, send_sem=k_sem.at[0], recv_sem=k_sem.at[1],
+        device_id={"seq": lax.rem(s + 1, seqs)}, device_id_type=MESH,
+    )
+    shift.start()
+    own_ref[...] = kvs[...]
+    query_ref[...] = acc[:, :key_at]
+    shift.wait()
+    prev_ref[...] = kvr[...]
+
+
+def forward(feat, lng, route, place, image, rgain, cosine, sine, weights, proj, text):
+    seqs, tps = lax.axis_size("seq"), lax.axis_size("tp")
+    own_rows, feats = feat.shape
+    vis = own_rows * seqs
+    tok = vis // tps
+    rows = text.shape[0]
+    width = weights[0].shape[0]
+    query_cols = weights[0].shape[1]
+    kv_cols = 2 * weights[1].shape[1]
+    cols = query_cols + kv_cols
+    heads = query_cols // HEAD
+    bf, f32 = jnp.bfloat16, jnp.float32
+    sem = pltpu.SemaphoreType.DMA
+    vm = pl.BlockSpec(memory_space=pltpu.VMEM)
+    hb = pl.BlockSpec(memory_space=pl.ANY)
+    moves = 11 if seqs == 8 else seqs - 1
+    return pl.pallas_call(
+        functools.partial(forward_kernel, seqs, tps, heads),
+        out_shape=(
+            jax.ShapeDtypeStruct((rows, query_cols), f32),
+            jax.ShapeDtypeStruct((rows, kv_cols), bf),
+            jax.ShapeDtypeStruct((rows, kv_cols), bf),
+            jax.ShapeDtypeStruct((vis, width), bf),
+            jax.ShapeDtypeStruct((own_rows, feats), f32),
+            jax.ShapeDtypeStruct((own_rows, HEAD), f32),
+        ),
+        in_specs=[vm] * 8 + [hb] * 5,
+        out_specs=(vm,) * 6,
+        scratch_shapes=[
+            pltpu.VMEM((seqs, width, cols), bf),
+            pltpu.VMEM((feats, width), bf),
+            pltpu.VMEM(text.shape, bf),
+            pltpu.VMEM((rows, cols), f32),
+            pltpu.VMEM((seqs, own_rows, feats), bf),
+            pltpu.VMEM((own_rows, HEAD), f32),
+            pltpu.VMEM((tps - 1, own_rows, HEAD), f32),
+            pltpu.VMEM((vis, width), f32),
+            pltpu.VMEM((tps - 1, tok, width), f32),
+            pltpu.VMEM((tps, tok, width), bf),
+            pltpu.VMEM((seqs, CAPD, width), bf),
+            pltpu.VMEM((seqs, CAPD, width), bf),
+            pltpu.VMEM((rows, kv_cols), bf),
+            pltpu.VMEM((rows, kv_cols), bf),
+            sem((5,)),
+            sem((moves,)),
+            sem((moves,)),
+            sem((tps - 1,)),
+            sem((tps - 1,)),
+            sem((seqs - 1,)),
+            sem((seqs - 1,)),
+            sem((tps - 1,)),
+            sem((tps - 1,)),
+            sem((tps - 1,)),
+            sem((tps - 1,)),
+            sem((seqs - 1,)),
+            sem((seqs - 1,)),
+            sem((2,)),
+        ],
+        compiler_params=pltpu.CompilerParams(
+            collective_id=1, has_side_effects=True, vmem_limit_bytes=VMEM_LIMIT
+        ),
+    )(feat, lng, route, place, image, rgain, cosine, sine, *weights, proj, text)
+
+
 def backward_kernel(
     seqs, tps, heads,
     qg_ref, og_ref, pg_ref, cos_ref, sin_ref, pick_ref, route_ref, emb_ref, gain_ref,
-    cen_ref, lng_ref, istd_ref, w_hbm, proj_hbm,
+    cen_ref, lng_ref, istd_ref, wq_hbm, wk_hbm, wv_hbm, proj_hbm,
     out_ref,
     w_ref, proj_ref, back, pre, gath, part, psend, precv, stat, srecv, eg, fsend, frecv, vstat,
     vrecv, local_sem, back_sem, g_send, g_recv, p_send, p_recv, s_send, s_recv, e_send, e_recv,
@@ -172,22 +441,13 @@
     own_rows = vis // seqs
     width = w_ref.shape[0]
     feats = proj_ref.shape[0]
-    load_w = pltpu.make_async_copy(w_hbm, w_ref, local_sem.at[0])
-    load_proj = pltpu.make_async_copy(proj_hbm, proj_ref, local_sem.at[1])
-    load_w.start()
+    load_w = weight_loads((wq_hbm, wk_hbm, wv_hbm), w_ref, local_sem)
+    load_proj = pltpu.make_async_copy(proj_hbm, proj_ref, local_sem.at[3])
+    for load in load_w:
+        load.start()
     load_proj.start()
 
-    barrier = pltpu.get_barrier_semaphore()
-    for step in range(1, seqs):
-        pl.semaphore_signal(
-            barrier, inc=1, device_id={"seq": lax.rem(s + step, seqs)}, device_id_type=MESH
-        )
-    for step in range(1, tps):
-        pl.semaphore_signal(
-            barrier, inc=1, device_id={"tp": lax.rem(t + step, tps)}, device_id_type=MESH
-        )
-    pl.semaphore_wait(barrier, seqs - 1 + tps - 1)
-
+    greet(seqs, tps, s, t)
     shift = pltpu.make_async_remote_copy(
         src_ref=pg_ref, dst_ref=back, send_sem=back_sem.at[0], recv_sem=back_sem.at[1],
         device_id={"seq": lax.rem(s + seqs - 1, seqs)}, device_id_type=MESH,
@@ -214,7 +474,8 @@
     copies = exchange(
         "seq", seqs, s, lambda peer: gath.at[0], lambda step: gath.at[step], g_send, g_recv
     )
-    load_w.wait()
+    for load in load_w:
+        load.wait()
     for copy in copies:
         copy.wait()
     slots = gath[...].reshape(seqs * CAPD, gath.shape[2])
@@ -286,11 +547,12 @@
     out_ref[...] = (istd_ref[...] * (scaled - mean - centred * inner)).astype(jnp.bfloat16)
 
 
-def backward(qg, og, pg, cosine, sine, pick, route, emb, gain, centred, lng, istd, w, proj, heads):
+def backward(qg, og, pg, cosine, sine, pick, route, emb, gain, centred, lng, istd, weights, proj, heads):
     seqs, tps = lax.axis_size("seq"), lax.axis_size("tp")
     vis = route.shape[0]
     tok, own_rows = vis // tps, vis // seqs
-    width, cols = w.shape
+    width = weights[0].shape[0]
+    cols = sum(w.shape[1] for w in weights)
     feats = proj.shape[0]
     bf, f32 = jnp.bfloat16, jnp.float32
     sem = pltpu.SemaphoreType.DMA
@@ -299,7 +561,7 @@
     return pl.pallas_call(
         functools.partial(backward_kernel, seqs, tps, heads),
         out_shape=jax.ShapeDtypeStruct((own_rows, feats), bf),
-        in_specs=[vm] * 12 + [hb] * 2,
+        in_specs=[vm] * 12 + [hb] * 4,
         out_specs=vm,
         scratch_shapes=[
             pltpu.VMEM((width, cols), bf),
@@ -317,7 +579,7 @@
             pltpu.VMEM((seqs - 1, own_rows, feats), bf),
             pltpu.VMEM((own_rows, HEAD), f32),
             pltpu.VMEM((tps - 1, own_rows, HEAD), f32),
-            sem((2,)),
+            sem((4,)),
             sem((2,)),
             sem((seqs - 1,)),
             sem((seqs - 1,)),
@@ -335,7 +597,7 @@
         compiler_params=pltpu.CompilerParams(
             collective_id=0, has_side_effects=True, vmem_limit_bytes=VMEM_LIMIT
         ),
-    )(qg, og, pg, cosine, sine, pick, route, emb, gain, centred, lng, istd, w, proj)
+    )(qg, og, pg, cosine, sine, pick, route, emb, gain, centred, lng, istd, *weights, proj)
 
 
 def on_device(
@@ -357,56 +619,32 @@
     my_index = lax.axis_index("seq")
     tok_rows = text_embed.shape[0]
     slot_cols = proj_weight.shape[1]
-    features = vis_feat.astype(jnp.float32)
-    row_total, row_squares = lax.psum(
-        (jnp.sum(features, axis=1), jnp.sum(features * features, axis=1)), "tp"
-    )
-    row_mean = row_total / VF
-    row_var = row_squares / VF - row_mean * row_mean
-    inv_std = lax.rsqrt(row_var + ln_eps)
-    centred = (features - row_mean[:, None]) * inv_std[:, None]
-    vis_normed = (centred * ln_gain[None, :]).astype(jnp.bfloat16)
-    partial_embed = jnp.dot(
-        lax.all_gather(vis_normed, "seq", axis=0, tiled=True),
-        proj_weight,
-        preferred_element_type=jnp.float32,
-    )
-    slot_live = (slot_token >= 0)[:, None]
-    slot_index = jnp.maximum(slot_token, 0)
-    summed = lax.psum(partial_embed, "tp")
-    embed = summed.astype(jnp.bfloat16)
-    embed_rows = jnp.take(embed, slot_index, axis=0)
-    outgoing = jnp.where(slot_live, embed_rows, jnp.zeros_like(embed_rows)).reshape(
-        seq_count, CAPD, slot_cols
-    )
-    arrived = lax.all_to_all(outgoing, "seq", split_axis=0, concat_axis=2, tiled=True)[0]
-    lanes = jnp.arange(CAPD, dtype=jnp.int32)
-    one_hot = (vis_slot[:, None] == lanes[None, :]).astype(jnp.bfloat16)
-    placed = jnp.dot(one_hot, arrived, preferred_element_type=jnp.float32).astype(jnp.bfloat16)
-    is_image = vis_slot >= 0
-    hidden = jnp.where(is_image[:, None], placed, text_embed)
-    hidden_wide = hidden.astype(jnp.float32)
-    inv_rms = lax.rsqrt(jnp.mean(hidden_wide * hidden_wide, axis=1, keepdims=True) + rms_eps)
-    normed = (hidden_wide * inv_rms * rms_gain[None, :]).astype(jnp.bfloat16)
-    stacked = jnp.concatenate([wq, wk, wv], axis=1)
     query_cols = wq.shape[1]
-    key_cols = wk.shape[1]
-    gathered = lax.all_gather(stacked, "seq", axis=0, tiled=True)
-    projected = jnp.dot(normed, gathered, preferred_element_type=jnp.float32)
     heads = query_cols // HEAD
-    groups = key_cols // HEAD
     positions = my_index * tok_rows + jnp.arange(tok_rows, dtype=jnp.int32)
     cosine, sine = rope_rows(positions)
-    pieces = []
-    for group in range(groups):
-        wide = projected[:, query_cols + group * HEAD : query_cols + (group + 1) * HEAD]
-        turned = jnp.concatenate([wide[:, HEAD // 2 :], wide[:, : HEAD // 2]], axis=1)
-        pieces.append((wide * cosine + turned * sine).astype(jnp.bfloat16))
-    pieces.append(projected[:, query_cols + key_cols :].astype(jnp.bfloat16))
-    own = jnp.concatenate(pieces, axis=1)
+    tail = tok_rows - CAPD
+    lanes = jnp.arange(CAPD, dtype=jnp.int32)
+    pick = (lanes[:, None] == vis_slot[None, tail:]).astype(jnp.bfloat16)
+    place = (vis_slot[tail:, None] == lanes[None, :]).astype(jnp.bfloat16)
+    image = (vis_slot[tail:, None] >= 0).astype(jnp.float32)
+    tokens = jnp.arange(token_slot.shape[0], dtype=jnp.int32)
+    out_route = (slot_token[:, None] == tokens[None, :]).astype(jnp.bfloat16)
     doc_marks = (doc_ids + 1).astype(jnp.bfloat16)
     prev_docs = shifted(doc_marks, "seq", 1)
-    prev = shifted(own, "seq", 1)
+    projected, own, prev, embed, centred, inv_std = forward(
+        vis_feat,
+        ln_gain[None, :],
+        out_route,
+        place,
+        image,
+        rms_gain[None, :],
+        cosine,
+        sine,
+        (wq, wk, wv),
+        proj_weight,
+        text_embed,
+    )
     query_docs = doc_marks.astype(jnp.float32)
     context, query_grads, own_grads, prev_grads = attention(
         projected,
@@ -420,8 +658,6 @@
         sine,
         heads,
     )
-    tail = tok_rows - CAPD
-    pick = (lanes[:, None] == vis_slot[None, tail:]).astype(jnp.bfloat16)
     slot_ids = jnp.arange(seq_count * CAPD, dtype=jnp.int32)
     source = (my_index - slot_ids // CAPD + seq_count) % seq_count
     held = source * CAPD + slot_ids % CAPD
@@ -439,8 +675,8 @@
         gain[None, :],
         centred,
         ln_gain[None, :],
-        inv_std[:, None],
-        stacked,
+        inv_std[:, :1],
+        (wq, wk, wv),
         proj_weight,
         heads,
     )

time: 243 us -> 240 us (0.988)
  Pallas kernels: 65.3 us -> 223 us
  waiting for transfers between devices: 59.4 us -> 0.01 us
  blocking collectives: 56.8 us -> 0 us
  matrix products: 22 us -> 0 us
  between operations: 14.4 us -> 0.7 us
  starting transfers between devices: 8.18 us -> 2.34 us
  local copies, waits for them, and re-layouts: 10.1 us -> 6.37 us
    pallas_call x0 -> x1, Pallas kernels: none -> 159 us  [forward(): pl.pallas_call(functools.partial(forward_kernel, seqs, tps, heads), out_s...]
    all_gather x1 -> x0, waiting for transfers between devices: 48 us -> none  [on_device(): gathered = lax.all_gather(stacked, 'seq', axis=0, tiled=True)]
    psum x2 -> x0, blocking collectives: 41.8 us -> none  [the longest x1 28.3 us: on_device(): summed = lax.psum(partial_embed, 'tp')]
    dot_general x3 -> x0, matrix products: 22 us -> none  [the longest x1 12.8 us: on_device(): projected = jnp.dot(normed, gathered, preferred_element_type=jnp.float32)]
    all_gather x1 -> x0, blocking collectives: 15.1 us -> none  [on_device(): lax.all_gather(vis_normed, 'seq', axis=0, tiled=True)]
    all_to_all x1 -> x0, waiting for transfers between devices: 11.3 us -> none  [on_device(): lax.all_to_all(outgoing, 'seq', split_axis=0, concat_axis=2, tiled=True)[0]]
    unnamed x36 -> x3, local copies, waits for them, and re-layouts: 5.84 us -> 1.55 us
    all_to_all x1 -> x0, starting transfers between devices: 3.49 us -> none  [on_device(): lax.all_to_all(outgoing, 'seq', split_axis=0, concat_axis=2, tiled=True)[0]]
  transfers between devices with their start and end apart: 4 -> 1, of which waited for: 2 -> 0; matrix products, arithmetic and copies ran while one was open for 13% -> 5% of each run, Pallas kernels for 0% -> 66%
where the time goes in v2:
time: 240 us
  Pallas kernels  223 us (93%)
  other arithmetic  7.54 us (3%)
  local copies, waits for them, and re-layouts  6.37 us (3%)
    pallas_call x1, Pallas kernels, forward(): pl.pallas_call(functools.partial(forward_kernel, seqs, tps, heads), out_s...  159 us
    pallas_call x1, Pallas kernels, backward(): pl.pallas_call(functools.partial(backward_kernel, seqs, tps, heads), out_...  53.3 us
    pallas_call x1, Pallas kernels, attention(): pl.pallas_call(functools.partial(attention_kernel, heads), out_shape=(jax...  10.9 us
  transfers between devices with their start and end apart: 1, of which 0 were waited for; matrix products, arithmetic and copies ran while one was open for 5% of the time, Pallas kernels for 66%

profile of v2, /device:TPU:0, one launch (start us, length us, event | category | flops | bytes accessed | tf_op | source)
XLA Modules:
  0.0 239.9 jit_solution(16327681220321511635)
XLA Ops:
  0.6 0.7 fusion.14
  1.3 0.0 copy-start
  1.3 2.3 collective-permute-start
  3.7 0.8 fusion.13
  4.4 0.7 slice.14
  5.2 0.5 fusion.1
  5.8 0.7 fusion.2
  6.5 0.8 pad_maximum_fusion
  7.3 1.3 broadcast_in_dim.14.lng_ref
  8.6 0.7 copy.16.image_ref
  9.3 0.7 fusion.5
  10.0 1.4 fusion.route_ref
  11.4 0.8 copy.17.qdoc_ref
  12.2 1.3 dynamic_slice.3
  13.4 1.4 compare_convert_fusion.route_ref
  14.8 158.7 %shard_map.140 = (f32[256,1024]{1,0:T(8,128)}, bf16[256,512]{1,0:T(8,128)(2,1)}, bf16[256,512]{1,0:T(8,128)(2,1)}, bf16[128,1024]{1,0:T(8,128)(2,1)}, f32[16,3200]{1,0:T(8,128)}, /*index=5*/f32[16,128]{1,0:T(8,128)}) custom-call(bf16[16,3200]{1,0:T(8,128)(2,1)} %feat_ref.1, f32[1,3200]{1,0:T(1,128)} %broadcast_in_dim.14.lng_ref, ...), custom_call_target="tpu_custom_call" | custom-call | tf_op jit(solution)/shard_map/pallas_call | solution.py:380
  173.6 0.0 copy-done
  173.6 0.0 collective-permute-done
  173.6 0.6 broadcast_in_dim.39
  174.2 10.9 %shard_map.141 = (bf16[256,1024]{1,0:T(8,128)(2,1)}, f32[32,1024]{1,0:T(8,128)}, f32[32,512]{1,0:T(8,128)}, bf16[32,512]{1,0:T(8,128)(2,1)}) custom-call(f32[256,1024]{1,0:T(8,128)} %get-tuple-element.12.proj_ref, bf16[256,512]{1,0:T(8,128)(2,1)} %get-tuple-element.13.own_ref, bf16[256,512]{1,0:T(8,128)(2,1)} %get-tuple-element.14.prev_ref, ...), custom_call_target="tpu_custom_call" | custom-call | tf_op jit(solution)/shard_map/pallas_call | solution.py:117
  185.1 53.3 %shard_map.142 = bf16[16,3200]{1,0:T(8,128)(2,1)} custom-call(f32[32,1024]{1,0:T(8,128)} %get-tuple-element.16.qg_ref, f32[32,512]{1,0:T(8,128)} %get-tuple-element.17.og_ref, bf16[32,512]{1,0:T(8,128)(2,1)} %get-tuple-element.18.pg_ref, f32[32,128]{1,0:T(8,128)} %get-tuple-element.32.cos_ref, f32[32,128]{1,0:T(8,128)} %get-tuple-element.31.sin_ref, ...), custom_call_target="tpu_custom_call" | custom-call | tf_op jit(solution)/shard_map/pallas_call | solution.py:561
  238.4 1.5 copy.19
  (3 shorter events, 0.0 us)
Async XLA Ops:
  1.3 172.3 %copy-start = (f32[256]{0:T(256)}, f32[256]{0:T(256)S(1)}, u32[]{:S(2)}) copy-start(f32[256]{0:T(256)S(1)} %get-tuple-element.22) | copy-start | bytes 3076
  1.3 172.3 %collective-permute-start = (bf16[256]{0:T(256)(128)(2,1)S(1)}, bf16[256]{0:T(256)(128)(2,1)S(1)}, u32[]{:S(2)}, u32[]{:S(2)}) collective-permute-start(bf16[256]{0:T(256)(128)(2,1)S(1)} %get-tuple-element.23), channel_id=1, source_target_pairs={{0,4},{4,8},{8,12},{12,16},{16,20},{20,24},{24,28},{1,5},{5,9},{9,... | collective-permute-start | bytes 1544 | tf_op jit(solution)/shard_map/ppermute | solution.py:26

commit v3 on v2

--- a/solution.py
+++ b/solution.py
@@ -182,7 +182,7 @@
 
 def forward_kernel(
     seqs, tps, heads,
-    feat_ref, lng_ref, route_ref, place_ref, image_ref, rgain_ref, cos_ref, sin_ref,
+    feat_ref, lng_ref, route_ref, pick_ref, rgain_ref, cos_ref, sin_ref,
     wq_hbm, wk_hbm, wv_hbm, proj_hbm, text_hbm,
     query_ref, own_ref, prev_ref, emb_ref, cen_ref, istd_ref,
     gw, proj_ref, hid, acc, nrm, stat, vrecv, part, precv, emb_s, out_s, arr, kvs, kvr,
@@ -205,8 +205,6 @@
     load_proj.start()
     load_text.start()
     greet(seqs, tps, s, t)
-    for load in loads:
-        load.wait()
 
     def other(bits):
         low, mid, high = s % 2, (s // 2) % 2, s // 4
@@ -229,17 +227,6 @@
         return copy
 
     grid = seqs == 8
-    if grid:
-        x_a = send(0, s, 0, 2)
-        y_b = send(1, s, 1, 4)
-        x_b = send(2, s, 1, 2)
-        y_a = send(3, s, 0, 4)
-        core = send(4, s, None, 1)
-    else:
-        spread = exchange(
-            "seq", seqs, s, lambda peer: gw.at[s], lambda step: gw.at[s], w_send, w_recv
-        )
-
     features = feat_ref[...].astype(jnp.float32)
     lane = lax.broadcasted_iota(jnp.int32, (own_rows, HEAD), 1)
     stat[...] = both_sums(features, features * features, lane)
@@ -258,6 +245,16 @@
     istd_ref[...] = jnp.broadcast_to(inv_std, istd_ref.shape)
     nrm[s] = (centred * lng_ref[...]).astype(jnp.bfloat16)
     copies = exchange("seq", seqs, s, lambda peer: nrm.at[s], lambda step: nrm.at[s], n_send, n_recv)
+    for load in loads:
+        load.wait()
+    if grid:
+        x_a = send(0, s, 0, 2)
+        y_b = send(1, s, 1, 4)
+        core = send(4, s, None, 1)
+    else:
+        spread = exchange(
+            "seq", seqs, s, lambda peer: gw.at[s], lambda step: gw.at[s], w_send, w_recv
+        )
     load_proj.wait()
     for copy in copies:
         copy.wait()
@@ -293,17 +290,20 @@
         "seq", seqs, s, lambda peer: out_s.at[peer], lambda step: arr.at[s], a_send, a_recv
     )
     if grid:
+        x_b = send(2, s, 1, 2)
+        y_a = send(3, s, 0, 4)
         x_a.wait()
         turn_y = send(5, other(2), 0, 4)
         y_b.wait()
         turn_x = send(6, other(4), 1, 2)
     for copy in copies:
         copy.wait()
-    image = image_ref[...] > 0.0
+    pick = pick_ref[...]
+    image = mul(pick, jnp.ones((CAPD, HEAD), jnp.bfloat16), TN)[:, :1] > 0.5
     square = jnp.zeros((rows, 1), jnp.float32)
     for index in range(seqs):
         cols = slice(index * width, (index + 1) * width)
-        placed = mul(place_ref[...], arr[index])
+        placed = mul(pick, arr[index], TN)
         text = hid[tail:, cols].astype(jnp.float32)
         hid[tail:, cols] = jnp.where(image, placed, text).astype(jnp.bfloat16)
         wide = hid[:, cols].astype(jnp.float32)
@@ -361,7 +361,7 @@
     prev_ref[...] = kvr[...]
 
 
-def forward(feat, lng, route, place, image, rgain, cosine, sine, weights, proj, text):
+def forward(feat, lng, route, pick, rgain, cosine, sine, weights, proj, text):
     seqs, tps = lax.axis_size("seq"), lax.axis_size("tp")
     own_rows, feats = feat.shape
     vis = own_rows * seqs
@@ -387,7 +387,7 @@
             jax.ShapeDtypeStruct((own_rows, feats), f32),
             jax.ShapeDtypeStruct((own_rows, HEAD), f32),
         ),
-        in_specs=[vm] * 8 + [hb] * 5,
+        in_specs=[vm] * 7 + [hb] * 5,
         out_specs=(vm,) * 6,
         scratch_shapes=[
             pltpu.VMEM((seqs, width, cols), bf),
@@ -422,7 +422,7 @@
         compiler_params=pltpu.CompilerParams(
             collective_id=1, has_side_effects=True, vmem_limit_bytes=VMEM_LIMIT
         ),
-    )(feat, lng, route, place, image, rgain, cosine, sine, *weights, proj, text)
+    )(feat, lng, route, pick, rgain, cosine, sine, *weights, proj, text)
 
 
 def backward_kernel(
@@ -436,7 +436,7 @@
 ):
     s, t = lax.axis_index("seq"), lax.axis_index("tp")
     groups = heads // GROUP
-    vis = route_ref.shape[0]
+    vis = route_ref.shape[1]
     tok = vis // tps
     own_rows = vis // seqs
     width = w_ref.shape[0]
@@ -469,17 +469,17 @@
         if group < groups:
             wide = unrotated(wide)
         pre[:, (heads + group) * HEAD : (heads + group + 1) * HEAD] = wide.astype(jnp.bfloat16)
-    gath[0] = mul(pick_ref[...], pre[...]).astype(jnp.bfloat16)
+    gath[s] = mul(pick_ref[...], pre[...]).astype(jnp.bfloat16)
 
     copies = exchange(
-        "seq", seqs, s, lambda peer: gath.at[0], lambda step: gath.at[step], g_send, g_recv
+        "seq", seqs, s, lambda peer: gath.at[s], lambda step: gath.at[s], g_send, g_recv
     )
     for load in load_w:
         load.wait()
     for copy in copies:
         copy.wait()
     slots = gath[...].reshape(seqs * CAPD, gath.shape[2])
-    selected = mul(route_ref[...], slots).astype(jnp.bfloat16)
+    selected = mul(route_ref[...], slots, TN).astype(jnp.bfloat16)
     part[...] = mul(selected, w_ref[...], NT)
     for step in range(1, tps):
         rows = pl.ds(pl.multiple_of(lax.rem(t + step, tps) * tok, 16), tok)
@@ -500,7 +500,7 @@
         copy.wait()
         norm_grads += precv[step].astype(jnp.float32)
     emb = emb_ref[mine, :].astype(jnp.float32)
-    scaled = norm_grads * gain_ref[...]
+    scaled = norm_grads * gain_ref[:, pl.ds(pl.multiple_of(s * width, HEAD), width)]
     lane = lax.broadcasted_iota(jnp.int32, (tok, HEAD), 1)
     stat[...] = both_sums(emb * emb, emb * scaled, lane)
     copies = exchange(
@@ -549,7 +549,7 @@
 
 def backward(qg, og, pg, cosine, sine, pick, route, emb, gain, centred, lng, istd, weights, proj, heads):
     seqs, tps = lax.axis_size("seq"), lax.axis_size("tp")
-    vis = route.shape[0]
+    vis = route.shape[1]
     tok, own_rows = vis // tps, vis // seqs
     width = weights[0].shape[0]
     cols = sum(w.shape[1] for w in weights)
@@ -626,8 +626,6 @@
     tail = tok_rows - CAPD
     lanes = jnp.arange(CAPD, dtype=jnp.int32)
     pick = (lanes[:, None] == vis_slot[None, tail:]).astype(jnp.bfloat16)
-    place = (vis_slot[tail:, None] == lanes[None, :]).astype(jnp.bfloat16)
-    image = (vis_slot[tail:, None] >= 0).astype(jnp.float32)
     tokens = jnp.arange(token_slot.shape[0], dtype=jnp.int32)
     out_route = (slot_token[:, None] == tokens[None, :]).astype(jnp.bfloat16)
     doc_marks = (doc_ids + 1).astype(jnp.bfloat16)
@@ -636,8 +634,7 @@
         vis_feat,
         ln_gain[None, :],
         out_route,
-        place,
-        image,
+        pick,
         rms_gain[None, :],
         cosine,
         sine,
@@ -658,11 +655,6 @@
         sine,
         heads,
     )
-    slot_ids = jnp.arange(seq_count * CAPD, dtype=jnp.int32)
-    source = (my_index - slot_ids // CAPD + seq_count) % seq_count
-    held = source * CAPD + slot_ids % CAPD
-    route = (token_slot[:, None] == held[None, :]).astype(jnp.bfloat16)
-    gain = lax.dynamic_slice_in_dim(rms_gain, my_index * slot_cols, slot_cols, 0)
     vis_grad = backward(
         query_grads,
         own_grads,
@@ -670,9 +662,9 @@
         cosine[tail:],
         sine[tail:],
         pick,
-        route,
+        out_route,
         embed,
-        gain[None, :],
+        rms_gain[None, :],
         centred,
         ln_gain[None, :],
         inv_std[:, :1],

time: 240 us -> 217 us (0.904)
  Pallas kernels: 223 us -> 204 us
    pallas_call x1, Pallas kernels: 159 us -> 141 us  [forward(): pl.pallas_call(functools.partial(forward_kernel, seqs, tps, heads), out_s...]
  transfers between devices with their start and end apart: 1 -> 1, of which waited for: 0 -> 0; matrix products, arithmetic and copies ran while one was open for 5% -> 3% of each run, Pallas kernels for 66% -> 65%
where the time goes in v3:
time: 217 us
  Pallas kernels  204 us (94%)
  other arithmetic  5.36 us (2%)
  local copies, waits for them, and re-layouts  4.41 us (2%)
  starting transfers between devices  2.34 us (1%)
    pallas_call x1, Pallas kernels, forward(): pl.pallas_call(functools.partial(forward_kernel, seqs, tps, heads), out_s...  141 us
    pallas_call x1, Pallas kernels, backward(): pl.pallas_call(functools.partial(backward_kernel, seqs, tps, heads), out_...  52 us
    pallas_call x1, Pallas kernels, attention(): pl.pallas_call(functools.partial(attention_kernel, heads), out_shape=(jax...  10.9 us
  transfers between devices with their start and end apart: 1, of which 0 were waited for; matrix products, arithmetic and copies ran while one was open for 3% of the time, Pallas kernels for 65%

profile of v3, /device:TPU:0, one launch (start us, length us, event | category | flops | bytes accessed | tf_op | source)
XLA Modules:
  0.0 217.0 jit_solution(4963014538772423828)
XLA Ops:
  0.6 0.7 fusion.5
  1.3 0.0 copy-start
  1.3 2.3 %collective-permute-start = (bf16[256]{0:T(256)(128)(2,1)S(1)}, bf16[256]{0:T(256)(128)(2,1)S(1)}, u32[]{:S(2)}, u32[]{:S(2)}) collective-permute-start(bf16[256]{0:T(256)(128)(2,1)S(1)} %get-tuple-element.23), channel_id=1, source_target_pairs={{0,4},{4,8},{8,12},{12,16},{16,20},{20,24},{24,28},{1,5},{5,9},{9,... | collective-permute-start | bytes 1544 | tf_op jit(solution)/shard_map/ppermute | solution.py:26
  3.7 0.5 fusion.1
  4.2 0.7 fusion.2
  4.9 0.8 pad_maximum_fusion
  5.8 0.7 slice.12
  6.5 0.6 fusion.4.pick_ref
  7.1 1.3 broadcast_in_dim.12.lng_ref
  8.4 1.4 fusion.route_ref
  9.9 0.8 copy.14.qdoc_ref
  10.6 141.3 %shard_map.131 = (f32[256,1024]{1,0:T(8,128)}, bf16[256,512]{1,0:T(8,128)(2,1)}, bf16[256,512]{1,0:T(8,128)(2,1)}, bf16[128,1024]{1,0:T(8,128)(2,1)}, f32[16,3200]{1,0:T(8,128)}, /*index=5*/f32[16,128]{1,0:T(8,128)}) custom-call(bf16[16,3200]{1,0:T(8,128)(2,1)} %feat_ref.1, f32[1,3200]{1,0:T(1,128)} %broadcast_in_dim.12.lng_ref, ...), custom_call_target="tpu_custom_call" | custom-call | tf_op jit(solution)/shard_map/pallas_call | solution.py:380
  151.9 0.0 copy-done
  152.0 0.0 collective-permute-done
  152.0 0.6 broadcast_in_dim.31
  152.6 10.9 %shard_map.132 = (bf16[256,1024]{1,0:T(8,128)(2,1)}, f32[32,1024]{1,0:T(8,128)}, f32[32,512]{1,0:T(8,128)}, bf16[32,512]{1,0:T(8,128)(2,1)}) custom-call(f32[256,1024]{1,0:T(8,128)} %get-tuple-element.12.proj_ref, bf16[256,512]{1,0:T(8,128)(2,1)} %get-tuple-element.13.own_ref, bf16[256,512]{1,0:T(8,128)(2,1)} %get-tuple-element.14.prev_ref, ...), custom_call_target="tpu_custom_call" | custom-call | tf_op jit(solution)/shard_map/pallas_call | solution.py:117
  163.5 52.0 %shard_map.133 = bf16[16,3200]{1,0:T(8,128)(2,1)} custom-call(f32[32,1024]{1,0:T(8,128)} %get-tuple-element.16.qg_ref, f32[32,512]{1,0:T(8,128)} %get-tuple-element.17.og_ref, bf16[32,512]{1,0:T(8,128)(2,1)} %get-tuple-element.18.pg_ref, f32[32,128]{1,0:T(8,128)} %get-tuple-element.30.cos_ref, f32[32,128]{1,0:T(8,128)} %get-tuple-element.29.sin_ref, ...), custom_call_target="tpu_custom_call" | custom-call | tf_op jit(solution)/shard_map/pallas_call | solution.py:561
  215.5 1.5 copy.16
  (2 shorter events, 0.0 us)
Async XLA Ops:
  1.3 150.6 %copy-start = (f32[256]{0:T(256)}, f32[256]{0:T(256)S(1)}, u32[]{:S(2)}) copy-start(f32[256]{0:T(256)S(1)} %get-tuple-element.22) | copy-start | bytes 3076
  1.3 150.6 %collective-permute-start = (bf16[256]{0:T(256)(128)(2,1)S(1)}, bf16[256]{0:T(256)(128)(2,1)S(1)}, u32[]{:S(2)}, u32[]{:S(2)}) collective-permute-start(bf16[256]{0:T(256)(128)(2,1)S(1)} %get-tuple-element.23), channel_id=1, source_target_pairs={{0,4},{4,8},{8,12},{12,16},{16,20},{20,24},{24,28},{1,5},{5,9},{9,... | collective-permute-start | bytes 1544 | tf_op jit(solution)/shard_map/ppermute | solution.py:26

commit v4 on v3

--- a/solution.py
+++ b/solution.py
@@ -258,6 +258,9 @@
     load_proj.wait()
     for copy in copies:
         copy.wait()
+    if grid:
+        x_b = send(2, s, 1, 2)
+        y_a = send(3, s, 0, 4)
     part[...] = mul(nrm[...].reshape(vis, feats), proj_ref[...])
     copies = []
     for step in range(1, tps):
@@ -290,8 +293,6 @@
         "seq", seqs, s, lambda peer: out_s.at[peer], lambda step: arr.at[s], a_send, a_recv
     )
     if grid:
-        x_b = send(2, s, 1, 2)
-        y_a = send(3, s, 0, 4)
         x_a.wait()
         turn_y = send(5, other(2), 0, 4)
         y_b.wait()

time: 217 us -> 217 us (level)
  no operation moved by 1% of the time
where the time goes in v4:
time: 217 us
  Pallas kernels  204 us (94%)
  other arithmetic  5.36 us (2%)
  local copies, waits for them, and re-layouts  4.41 us (2%)
  starting transfers between devices  2.34 us (1%)
    pallas_call x1, Pallas kernels, forward(): pl.pallas_call(functools.partial(forward_kernel, seqs, tps, heads), out_s...  141 us
    pallas_call x1, Pallas kernels, backward(): pl.pallas_call(functools.partial(backward_kernel, seqs, tps, heads), out_...  52 us
    pallas_call x1, Pallas kernels, attention(): pl.pallas_call(functools.partial(attention_kernel, heads), out_shape=(jax...  10.9 us
  transfers between devices with their start and end apart: 1, of which 0 were waited for; matrix products, arithmetic and copies ran while one was open for 3% of the time, Pallas kernels for 65%

profile of v4, /device:TPU:0, one launch (start us, length us, event | category | flops | bytes accessed | tf_op | source)
XLA Modules:
  0.0 217.0 jit_solution(14552490856819338350)
XLA Ops:
  0.6 0.7 fusion.5
  1.3 0.0 copy-start
  1.3 2.3 %collective-permute-start = (bf16[256]{0:T(256)(128)(2,1)S(1)}, bf16[256]{0:T(256)(128)(2,1)S(1)}, u32[]{:S(2)}, u32[]{:S(2)}) collective-permute-start(bf16[256]{0:T(256)(128)(2,1)S(1)} %get-tuple-element.23), channel_id=1, source_target_pairs={{0,4},{4,8},{8,12},{12,16},{16,20},{20,24},{24,28},{1,5},{5,9},{9,... | collective-permute-start | bytes 1544 | tf_op jit(solution)/shard_map/ppermute | solution.py:26
  3.7 0.5 fusion.1
  4.2 0.7 fusion.2
  4.9 0.8 pad_maximum_fusion
  5.8 0.7 slice.12
  6.5 0.6 fusion.4.pick_ref
  7.1 1.3 broadcast_in_dim.12.lng_ref
  8.4 1.4 fusion.route_ref
  9.9 0.8 copy.14.qdoc_ref
  10.6 141.3 %shard_map.131 = (f32[256,1024]{1,0:T(8,128)}, bf16[256,512]{1,0:T(8,128)(2,1)}, bf16[256,512]{1,0:T(8,128)(2,1)}, bf16[128,1024]{1,0:T(8,128)(2,1)}, f32[16,3200]{1,0:T(8,128)}, /*index=5*/f32[16,128]{1,0:T(8,128)}) custom-call(bf16[16,3200]{1,0:T(8,128)(2,1)} %feat_ref.1, f32[1,3200]{1,0:T(1,128)} %broadcast_in_dim.12.lng_ref, ...), custom_call_target="tpu_custom_call" | custom-call | tf_op jit(solution)/shard_map/pallas_call | solution.py:381
  151.9 0.0 copy-done
  152.0 0.0 collective-permute-done
  152.0 0.6 broadcast_in_dim.31
  152.6 10.9 %shard_map.132 = (bf16[256,1024]{1,0:T(8,128)(2,1)}, f32[32,1024]{1,0:T(8,128)}, f32[32,512]{1,0:T(8,128)}, bf16[32,512]{1,0:T(8,128)(2,1)}) custom-call(f32[256,1024]{1,0:T(8,128)} %get-tuple-element.12.proj_ref, bf16[256,512]{1,0:T(8,128)(2,1)} %get-tuple-element.13.own_ref, bf16[256,512]{1,0:T(8,128)(2,1)} %get-tuple-element.14.prev_ref, ...), custom_call_target="tpu_custom_call" | custom-call | tf_op jit(solution)/shard_map/pallas_call | solution.py:117
  163.5 52.0 %shard_map.133 = bf16[16,3200]{1,0:T(8,128)(2,1)} custom-call(f32[32,1024]{1,0:T(8,128)} %get-tuple-element.16.qg_ref, f32[32,512]{1,0:T(8,128)} %get-tuple-element.17.og_ref, bf16[32,512]{1,0:T(8,128)(2,1)} %get-tuple-element.18.pg_ref, f32[32,128]{1,0:T(8,128)} %get-tuple-element.30.cos_ref, f32[32,128]{1,0:T(8,128)} %get-tuple-element.29.sin_ref, ...), custom_call_target="tpu_custom_call" | custom-call | tf_op jit(solution)/shard_map/pallas_call | solution.py:562
  215.5 1.5 copy.16
  (2 shorter events, 0.0 us)
Async XLA Ops:
  1.3 150.6 %copy-start = (f32[256]{0:T(256)}, f32[256]{0:T(256)S(1)}, u32[]{:S(2)}) copy-start(f32[256]{0:T(256)S(1)} %get-tuple-element.22) | copy-start | bytes 3076
  1.3 150.6 %collective-permute-start = (bf16[256]{0:T(256)(128)(2,1)S(1)}, bf16[256]{0:T(256)(128)(2,1)S(1)}, u32[]{:S(2)}, u32[]{:S(2)}) collective-permute-start(bf16[256]{0:T(256)(128)(2,1)S(1)} %get-tuple-element.23), channel_id=1, source_target_pairs={{0,4},{4,8},{8,12},{12,16},{16,20},{20,24},{24,28},{1,5},{5,9},{9,... | collective-permute-start | bytes 1544 | tf_op jit(solution)/shard_map/ppermute | solution.py:26
